TPU v7x, 256 devices: a whole 4x4x8 slice. The times are simulated.
256 devices in a mesh: rows: 8 (over z), cols: 32 (over x, y, core).
Axes of the slice: x: 4, y: 4, z: 8, core: 2. Of those that a mesh axis runs over, the one named last changes fastest.
Arguments:
- inputs: bfloat16 [64, 512, 192], P('rows', 'cols'), may hold values from -6 to 6
- step_sizes: bfloat16 [64, 512, 192], P('rows', 'cols'), may hold values from 0.5 to 2
- write_coef: bfloat16 [4, 64, 512, 16], P(None, 'rows', 'cols'), may hold values from -2 to 2
- read_coef: bfloat16 [4, 64, 512, 16], P(None, 'rows', 'cols'), may hold values from -2 to 2
- rate_table: float32 [4, 192, 16], replicated, may hold values from 0.00048828125 to 0.08
- skip_gain: float32 [192], replicated, may hold values from 0.5 to 2
- grad_out: bfloat16 [64, 512, 192], P('rows', 'cols'), may hold values from -6 to 6
Outputs:
- grad_inputs: float32 [64, 512, 192], P('rows', 'cols')
- grad_steps: float32 [64, 512, 192], P('rows', 'cols')
- grad_write: float32 [4, 64, 512, 16], P(None, 'rows', 'cols')
- grad_read: float32 [4, 64, 512, 16], P(None, 'rows', 'cols')
- grad_rates: float32 [4, 192, 16], replicated
- grad_skip: float32 [192], replicated
All inputs are finite; a program needn't handle non-finite values.
Results may differ from a plain program's by a relative error of at most 0.00045.
Values sent between devices are 32-bit elements; how exact they have to be, the bound alone decides.
A program may use at most 128 MiB of HBM per device.

v0:
```python
import functools
import math

import jax
import jax.numpy as jnp
from jax import lax
from jax.experimental import pallas as pl
from jax.experimental.pallas import tpu as pltpu
from jax.sharding import PartitionSpec as P

F32 = jnp.float32
T = 16
PAIRS = 8
LOG2E = 1.4426950408889634
LN2 = 0.6931471805599453
COLS = 32
ROWS = 8


def low_half():
    return lax.broadcasted_iota(jnp.int32, (8, 128), 1) < 64


def spread(coef, base, low):
    a = jnp.broadcast_to(coef[:, base : base + 1], (8, 128))
    b = jnp.broadcast_to(coef[:, base + 8 : base + 9], (8, 128))
    return a, b, jnp.where(low, a, b)


def fold(q, low):
    first = jnp.where(low, q[0], q[1])
    second = jnp.where(low, q[1], q[0])
    return first + pltpu.roll(second, 64, 1) + q[2]


def tri(f, *groups):
    return [f(*parts) for parts in zip(*groups)]


def add(a, b):
    return a + b


def mul(a, b):
    return a * b


def body(x_ref, s_ref, g_ref, w_ref, r_ref, rt_ref, sk_ref,
         gi_ref, gs_ref, gw_ref, gr_ref, fin_ref,
         flat, zmsg, rowtile, dat, coef, decays, ssend, srecv, csend, crecv, bsend, brecv,
         zrecv, keep, thr, mac, zbuf, place, th_nat, m_nat, zout, zback, asend, arecv, zsum,
         send_sem, recv_sem):
    col = lax.axis_index("cols")
    row = lax.axis_index("rows")
    low = low_half()

    barrier = pltpu.get_barrier_semaphore()

    def greet_cols(i, _):
        pl.semaphore_signal(barrier, inc=1, device_id={"cols": lax.rem(col + i, COLS)},
                            device_id_type=pl.DeviceIdType.MESH)
        return 0

    def greet_rows(i, _):
        pl.semaphore_signal(barrier, inc=1, device_id={"rows": lax.rem(row + i, ROWS)},
                            device_id_type=pl.DeviceIdType.MESH)
        return 0

    lax.fori_loop(1, COLS, greet_cols, 0)
    lax.fori_loop(1, ROWS, greet_rows, 0)

    for r in range(8):
        sv = s_ref[r].astype(F32)
        gv = g_ref[r].astype(F32)
        pv = sv * x_ref[r].astype(F32)
        at = pl.ds(r * 16, 16)
        flat[0, at, :] = sv[:, :128]
        flat[1, at, :] = pv[:, :128]
        flat[2, at, :] = gv[:, :128]
        flat[3, at, :] = jnp.concatenate([sv[:, 128:], pv[:, 128:]], axis=1)
        flat[4, at, :] = jnp.concatenate(
            [gv[:, 128:]] + [ref[k, r].astype(F32) for ref in (w_ref, r_ref) for k in (2, 3)], axis=1)
        flat[5, at, :] = jnp.concatenate(
            [gv[:, 128:]] + [ref[k, r].astype(F32) for ref in (w_ref, r_ref) for k in (0, 1)], axis=1)

    ssum = [jnp.zeros((8, 128), F32), jnp.zeros((8, 128), F32)]
    for t in range(T):
        at = pl.ds(t, 8, stride=16)
        for q in range(5):
            zmsg[q, t] = flat[q, at, :]
        rowtile[t] = flat[5, at, :]

    def unpack(t, tiles):
        s_lo, p_lo, g_lo, sp, gc = tiles
        spr = pltpu.roll(sp, 64, 1)
        gcr = pltpu.roll(gc, 64, 1)
        dat[0, t] = s_lo
        dat[1, t] = jnp.where(low, sp, spr)
        dat[2, t] = p_lo
        dat[3, t] = jnp.where(low, spr, sp)
        dat[4, t] = g_lo
        dat[5, t] = jnp.where(low, gc, gcr)
        coef[t] = gcr

    for t in range(T):
        unpack(t, (zmsg[0, t], zmsg[1, t], zmsg[2, t], zmsg[3, t], rowtile[t]))
        ssum = [ssum[0] + dat[0, t], ssum[1] + dat[1, t]]
    ssend[0] = ssum[0]
    ssend[1] = ssum[1]
    srecv[col] = ssend[...]

    pl.semaphore_wait(barrier, COLS - 1 + ROWS - 1)

    def remote(src, dst, n, **to):
        return pltpu.make_async_remote_copy(
            src_ref=src, dst_ref=dst, send_sem=send_sem.at[n], recv_sem=recv_sem.at[n],
            device_id=to, device_id_type=pl.DeviceIdType.MESH)

    def taken(ref, sem, n):
        pltpu.make_async_copy(ref, ref, sem.at[n]).wait()

    def send_z(i, _):
        to = lax.rem(row + i, ROWS)
        for c in range(2):
            remote(zmsg.at[:, 2 * to + c],
                   zrecv.at[:, pl.ds(pl.multiple_of(c * 64 + row * 8, 8), 8), :], 0, rows=to).start()
        return 0

    lax.fori_loop(1, ROWS, send_z, 0)
    for c in range(2):
        for q in range(5):
            zrecv[q, pl.ds(pl.multiple_of(c * 64 + row * 8, 8), 8), :] = zmsg[q, 2 * row + c]

    def send_s(i, _):
        to = lax.rem(col + i, COLS)
        remote(ssend, srecv.at[col], 1, cols=to).start()
        return 0

    lax.fori_loop(1, COLS, send_s, 0)

    def rates(k, p):
        return [jnp.broadcast_to(rt_ref[k, p, pl.ds(i, 1), :], (8, 128)) for i in range(3)]

    def load(q, t):
        lo = dat[2 * q, t]
        return [lo, lo, dat[2 * q + 1, t]]

    def coefs(t, p):
        return pltpu.roll(coef[t], lax.rem(128 - p, 128), 1)

    W_A, W_D, R_A, R_D = 0, 16, 32, 48
    zero3 = [jnp.zeros((8, 128), F32)] * 3

    def local_pass(p, slot, ka, kd):
        ra, rd = rates(ka, p), rates(kd, p)

        def up(t, carry):
            fa, md = carry[:3], carry[3:]
            s = load(0, t)
            da = tri(lambda a, b: jnp.exp2(a * b), s, ra)
            dd = tri(lambda a, b: jnp.exp2(a * b), s, rd)
            for i in range(3):
                decays[slot, t, i] = da[i]
                decays[slot, t, 3 + i] = dd[i]
            c = coefs(t, p)
            drive = tri(mul, load(1, t), spread(c, W_A, low))
            fa = tri(add, tri(mul, da, fa), drive)
            md = tri(mul, dd, tri(add, tri(mul, load(2, t), spread(c, R_D, low)), md))
            return (*fa, *md)

        def down(i, carry):
            t = T - 1 - i
            ma, fd = carry[:3], carry[3:]
            da = [decays[slot, t, i] for i in range(3)]
            dd = [decays[slot, t, 3 + i] for i in range(3)]
            c = coefs(t, p)
            drive = tri(mul, load(1, t), spread(c, W_D, low))
            fd = tri(add, tri(mul, dd, fd), drive)
            ma = tri(mul, da, tri(add, tri(mul, load(2, t), spread(c, R_A, low)), ma))
            return (*ma, *fd)

        a = lax.fori_loop(0, T, up, (*zero3, *zero3), unroll=True)
        b = lax.fori_loop(0, T, down, (*zero3, *zero3), unroll=True)
        return a[:3], b[:3], b[3:], a[3:]

    def final_pass(p, slot, ka, kd, starts):
        ra, rd = rates(ka, p), rates(kd, p)
        fa0, ma0, fd0, md0 = starts

        def up(t, carry):
            h, m = carry[:3], carry[3:]
            da = [decays[slot, t, i] for i in range(3)]
            dd = [decays[slot, t, 3 + i] for i in range(3)]
            sx, g = load(1, t), load(2, t)
            c = coefs(t, p)
            db = tri(mul, da, h)
            h = tri(add, db, tri(mul, sx, spread(c, W_A, low)))
            adj = tri(add, tri(mul, g, spread(c, R_D, low)), m)
            for i in range(3):
                keep[t, i] = db[i]
                keep[t, 3 + i] = adj[i]
            zbuf[2, p, t] = fold(tri(mul, h, g), low)
            zbuf[1, p, t] = fold(tri(mul, adj, sx), low)
            th = tri(mul, adj, spread(c, W_D, low))
            thr[0, t] += th[0] + th[1]
            thr[1, t] += th[2]
            return (*h, *tri(mul, dd, adj))

        def down(i, carry):
            t = T - 1 - i
            m, h, acc_a, acc_d = carry[:3], carry[3:6], carry[6:9], carry[9:]
            da = [decays[slot, t, i] for i in range(3)]
            dd = [decays[slot, t, 3 + i] for i in range(3)]
            s, sx, g = load(0, t), load(1, t), load(2, t)
            c = coefs(t, p)
            db = tri(mul, dd, h)
            h = tri(add, db, tri(mul, sx, spread(c, W_D, low)))
            adj = tri(add, tri(mul, g, spread(c, R_A, low)), m)
            zbuf[3, p, t] = fold(tri(mul, h, g), low)
            zbuf[0, p, t] = fold(tri(mul, adj, sx), low)
            th = tri(mul, adj, spread(c, W_A, low))
            thr[0, t] += th[0] + th[1]
            thr[1, t] += th[2]
            mem_a = tri(mul, adj, [keep[t, i] for i in range(3)])
            mem_d = tri(mul, [keep[t, 3 + i] for i in range(3)], db)
            mr = tri(add, tri(mul, mem_a, ra), tri(mul, mem_d, rd))
            mac[0, t] += mr[0] + mr[1]
            mac[1, t] += mr[2]
            acc_a = tri(add, acc_a, tri(mul, mem_a, s))
            acc_d = tri(add, acc_d, tri(mul, mem_d, s))
            return (*tri(mul, da, adj), *h, *acc_a, *acc_d)

        lax.fori_loop(0, T, up, (*fa0, *md0), unroll=True)
        out = lax.fori_loop(0, T, down, (*ma0, *fd0, *zero3, *zero3), unroll=True)
        for k, acc in ((ka, out[6:9]), (kd, out[9:])):
            for i in range(3):
                asend[k * PAIRS + p, pl.ds(i, 1), :] = -jnp.sum(acc[i], axis=0, keepdims=True)

    def clear():
        thr[...] = jnp.zeros_like(thr)
        mac[...] = jnp.zeros_like(mac)

    def channel_sums():
        total = None
        for q in range(4):
            whole = jnp.concatenate([zbuf[q, p].reshape(128, 128) for p in range(PAIRS)], axis=1)
            high = whole.astype(jnp.bfloat16)
            rest = (whole - high.astype(F32)).astype(jnp.bfloat16)
            part = jnp.dot(high, place[...], preferred_element_type=F32)
            part = part + jnp.dot(rest, place[...], preferred_element_type=F32)
            part = part if q == 0 else pltpu.roll(part, 16 * q, 1)
            total = part if total is None else total + part
        return total.reshape(T, 8, 128)

    def both_halves(v):
        return v + pltpu.roll(v, 64, 1)

    def row_local(p, _):
        fa, ma, fd, md = local_pass(p, p, 0, 1)
        for q, parts in enumerate((fa, ma, fd, md)):
            for i in range(3):
                csend[q * PAIRS + p, i] = parts[i]
        return 0

    lax.fori_loop(0, PAIRS, row_local, 0)

    def send_c(i, _):
        to = lax.rem(col + i, COLS)
        remote(csend.at[to], crecv.at[col], 2, cols=to).start()
        return 0

    lax.fori_loop(1, COLS, send_c, 0)
    crecv[col] = csend[col]

    spot_k = lax.broadcasted_iota(jnp.int32, (128, 128), 0) // 64 * 8
    spot_n = lax.broadcasted_iota(jnp.int32, (128, 128), 1)
    for p in range(PAIRS):
        place[pl.ds(p * 128, 128), :] = jnp.where(spot_n == spot_k + p, 1.0, 0.0).astype(jnp.bfloat16)
    skip = [jnp.zeros((1, 192), F32)]
    for r in range(8):
        skip[0] = skip[0] + jnp.sum(g_ref[r].astype(F32) * x_ref[r].astype(F32), axis=0, keepdims=True)
    skip_lo = skip[0][:, :128]
    skip_hi = jnp.concatenate([skip[0][:, 128:], skip[0][:, 128:]], axis=1)
    skip_tile = jnp.concatenate([jnp.zeros((3, 128), F32), skip_lo, skip_hi, jnp.zeros((3, 128), F32)], axis=0)

    def put_skip(o, _):
        asend[o] = skip_tile
        return 0

    lax.fori_loop(0, COLS, put_skip, 0)
    clear()

    taken(srecv.at[pl.ds(0, COLS - 1)], recv_sem, 1)
    taken(crecv.at[pl.ds(0, COLS - 1)], recv_sem, 2)
    kind = col // PAIRS
    pair = lax.rem(col, PAIRS)
    falls = jnp.where((kind == 1) | (kind == 2), 1, 0)
    own_rates = rates(kind // 2, pair)

    def chain(i, carry):
        b = i + falls * (COLS - 1 - 2 * i)
        for j in range(3):
            bsend[b, j] = carry[j]
        s_lo, s_hi = srecv[b, 0], srecv[b, 1]
        held = tri(lambda a, r: jnp.exp2(a * r), [s_lo, s_lo, s_hi], own_rates)
        return tuple(held[j] * carry[j] + crecv[b, j] for j in range(3))

    lax.fori_loop(0, COLS, chain, tuple(zero3), unroll=True)

    def send_b(i, _):
        to = lax.rem(col + i, COLS)
        remote(bsend.at[to], brecv.at[col], 3, cols=to).start()
        return 0

    lax.fori_loop(1, COLS, send_b, 0)
    brecv[col] = bsend[col]

    taken(brecv.at[pl.ds(0, COLS - 1)], recv_sem, 3)

    def row_final(p, _):
        starts = [[brecv[q * PAIRS + p, i] for i in range(3)] for q in range(4)]
        final_pass(p, p, 0, 1, starts)
        return 0

    lax.fori_loop(0, PAIRS, row_final, 0)
    sums = channel_sums()
    for t in range(T):
        at = pl.ds(t, 8, stride=16)
        th_nat[0, at, :] = thr[0, t]
        th_nat[1, at, :] = both_halves(thr[1, t])
        m_nat[0, at, :] = mac[0, t]
        m_nat[1, at, :] = both_halves(mac[1, t])
        flat[5, at, :] = sums[t]

    taken(zrecv.at[:, pl.ds(0, 112), :], recv_sem, 0)
    for t in range(T):
        at = pl.ds(t, 8, stride=16)
        unpack(t, [zrecv[q, at, :] for q in range(5)])
    zs = [jnp.zeros((8, 128), F32), jnp.zeros((8, 128), F32)]
    for t in range(T):
        zs = [zs[0] + dat[0, t], zs[1] + dat[1, t]]
    clear()
    chunk = lax.rem(lax.broadcasted_iota(jnp.int32, (8, 128), 0), 4)

    def line_final(p, carry):
        zs_lo, zs_hi = carry
        fa, ma, fd, md = local_pass(p, 0, 2, 3)
        ha = tri(lambda a, r: jnp.exp2(a * r), [zs_lo, zs_lo, zs_hi], rates(2, p))
        hd = tri(lambda a, r: jnp.exp2(a * r), [zs_lo, zs_lo, zs_hi], rates(3, p))

        def across(held, ends, rising):
            out = []
            for a, f in zip(held, ends):
                st = jnp.zeros((8, 128), F32)
                for _ in range(3):
                    moved = pltpu.roll(a * st + f, 1 if rising else 7, 0)
                    st = jnp.where(chunk > 0 if rising else chunk < 3, moved, 0.0)
                out.append(st)
            return out

        final_pass(p, 0, 2, 3, [across(ha, fa, True), across(ha, ma, False),
                                across(hd, fd, False), across(hd, md, True)])
        return carry

    lax.fori_loop(0, PAIRS, line_final, tuple(zs))
    sums = channel_sums()
    for t in range(T):
        at = pl.ds(t, 8, stride=16)
        zout[0, at, :] = thr[0, t]
        zout[1, at, :] = mac[0, t]
        zout[2, at, :] = jnp.where(low, both_halves(thr[1, t]), both_halves(mac[1, t]))
        zout[3, at, :] = sums[t]

    def send_back(i, _):
        to = lax.rem(row + i, ROWS)
        for c in range(2):
            remote(zout.at[:, pl.ds(pl.multiple_of(c * 64 + to * 8, 8), 8), :],
                   zback.at[:, pl.ds(pl.multiple_of(row * 16 + c * 8, 8), 8), :], 4, rows=to).start()
        return 0

    lax.fori_loop(1, ROWS, send_back, 0)
    for c in range(2):
        zback[:, pl.ds(pl.multiple_of(row * 16 + c * 8, 8), 8), :] = (
            zout[:, pl.ds(pl.multiple_of(c * 64 + row * 8, 8), 8), :])

    def send_a(i, _):
        to = lax.rem(col + i, COLS)
        remote(asend.at[to], arecv.at[col], 5, cols=to).start()
        return 0

    lax.fori_loop(1, COLS, send_a, 0)
    arecv[col] = asend[col]
    taken(arecv.at[pl.ds(0, COLS - 1)], recv_sem, 5)
    total = arecv[0]
    for b in range(1, COLS):
        total = total + arecv[b]
    zsum[row] = total

    def send_zsum(i, _):
        to = lax.rem(row + i, ROWS)
        remote(zsum.at[row], zsum.at[row], 6, rows=to).start()
        return 0

    lax.fori_loop(1, ROWS, send_zsum, 0)

    taken(zback.at[:, pl.ds(0, 112), :], recv_sem, 4)
    for r in range(8):
        back = pl.ds(r, 16, stride=8)
        at = pl.ds(r * 16, 16)
        packed = zback[2, back, :]
        th_lo = th_nat[0, at, :] + zback[0, back, :]
        m_lo = m_nat[0, at, :] + zback[1, back, :]
        th_hi = (th_nat[1, at, :] + packed)[:, :64]
        m_hi = (m_nat[1, at, :] + pltpu.roll(packed, 64, 1))[:, :64]
        xv = x_ref[r].astype(F32)
        sv = s_ref[r].astype(F32)
        gv = g_ref[r].astype(F32)
        gi_ref[r, :, :128] = sk_ref[:, :128] * gv[:, :128] + sv[:, :128] * th_lo
        gi_ref[r, :, 128:] = sk_ref[:, 128:] * gv[:, 128:] + sv[:, 128:] * th_hi
        gs_ref[r, :, :128] = th_lo * xv[:, :128] + LN2 * m_lo
        gs_ref[r, :, 128:] = th_hi * xv[:, 128:] + LN2 * m_hi
        mine = flat[5, at, :]
        other = zback[3, back, :]
        gw_ref[0, r] = mine[:, :16]
        gw_ref[1, r] = mine[:, 16:32]
        gr_ref[0, r] = mine[:, 32:48]
        gr_ref[1, r] = mine[:, 48:64]
        gw_ref[2, r] = other[:, :16]
        gw_ref[3, r] = other[:, 16:32]
        gr_ref[2, r] = other[:, 32:48]
        gr_ref[3, r] = other[:, 48:64]

    pltpu.make_async_copy(zsum.at[pl.ds(0, ROWS - 1)], zsum.at[pl.ds(0, ROWS - 1)], recv_sem.at[6]).wait()
    total = zsum[0]
    for b in range(1, ROWS):
        total = total + zsum[b]
    fin_ref[col] = total

    def send_fin(i, _):
        to = lax.rem(col + i, COLS)
        remote(fin_ref.at[col], fin_ref.at[col], 7, cols=to).start()
        return 0

    lax.fori_loop(1, COLS, send_fin, 0)
    taken(fin_ref.at[pl.ds(0, COLS - 1)], recv_sem, 7)

    taken(zrecv.at[:, pl.ds(0, 112), :], send_sem, 0)
    taken(srecv.at[pl.ds(0, COLS - 1)], send_sem, 1)
    taken(crecv.at[pl.ds(0, COLS - 1)], send_sem, 2)
    taken(brecv.at[pl.ds(0, COLS - 1)], send_sem, 3)
    taken(zback.at[:, pl.ds(0, 112), :], send_sem, 4)
    taken(arecv.at[pl.ds(0, COLS - 1)], send_sem, 5)
    taken(zsum.at[pl.ds(0, ROWS - 1)], send_sem, 6)
    taken(fin_ref.at[pl.ds(0, COLS - 1)], send_sem, 7)


def on_device(inputs, step_sizes, write_coef, read_coef, rate_table, skip_gain, grad_out):
    by_state = (rate_table * (-LOG2E)).transpose(0, 2, 1)
    lo = by_state[:, :, :128].reshape(4, 2, 8, 128)
    hi = by_state[:, :, 128:].reshape(4, 2, 8, 64)
    table = jnp.stack([lo[:, 0], lo[:, 1], jnp.concatenate([hi[:, 0], hi[:, 1]], axis=-1)], axis=2)
    vm = pl.BlockSpec(memory_space=pltpu.VMEM)
    shapes = [
        (6, 128, 128),
        (5, T, 8, 128),
        (T, 8, 128),
        (6, T, 8, 128),
        (T, 8, 128),
        (PAIRS, T, 6, 8, 128),
        (2, 8, 128),
        (COLS, 2, 8, 128),
        (COLS, 3, 8, 128),
        (COLS, 3, 8, 128),
        (COLS, 3, 8, 128),
        (COLS, 3, 8, 128),
        (5, 128, 128),
        (T, 6, 8, 128),
        (2, T, 8, 128),
        (2, T, 8, 128),
        (4, PAIRS, T, 8, 128),
        None,
        (2, 128, 128),
        (2, 128, 128),
        (4, 128, 128),
        (4, 128, 128),
        (COLS, 8, 128),
        (COLS, 8, 128),
        (ROWS, 8, 128),
    ]
    scratch = [pltpu.VMEM((PAIRS * 128, 128), jnp.bfloat16) if s is None else pltpu.VMEM(s, F32) for s in shapes]
    scratch += [pltpu.SemaphoreType.DMA((8,)), pltpu.SemaphoreType.DMA((8,))]
    gi, gs, gw, gr, fin = pl.pallas_call(
        body,
        out_shape=[
            jax.ShapeDtypeStruct((8, 16, 192), F32),
            jax.ShapeDtypeStruct((8, 16, 192), F32),
            jax.ShapeDtypeStruct((4, 8, 16, 16), F32),
            jax.ShapeDtypeStruct((4, 8, 16, 16), F32),
            jax.ShapeDtypeStruct((COLS, 8, 128), F32),
        ],
        in_specs=[vm] * 7,
        out_specs=[vm] * 5,
        scratch_shapes=scratch,
        compiler_params=pltpu.CompilerParams(
            collective_id=0, has_side_effects=True, vmem_limit_bytes=32 * 1024 * 1024),
    )(inputs, step_sizes, grad_out, write_coef, read_coef, table, skip_gain.reshape(1, 192))
    parts = fin.reshape(4, 8, 8, 128)
    lo = parts[:, :, :2].transpose(0, 3, 2, 1).reshape(4, 128, 16)
    hi = parts[:, :, 2].reshape(4, 8, 2, 64).transpose(0, 3, 2, 1).reshape(4, 64, 16)
    grad_rates = jnp.concatenate([lo, hi], axis=1)
    grad_skip = jnp.concatenate([fin[0, 3], fin[0, 4, :64]])
    return gi, gs, gw, gr, grad_rates, grad_skip


def solution(mesh):
    cells, coefs = P("rows", "cols", None), P(None, "rows", "cols", None)
    return jax.shard_map(
        on_device, mesh=mesh, in_specs=(cells, cells, coefs, coefs, P(), P(), cells),
        out_specs=(cells, cells, coefs, coefs, P(), P()), check_vma=False)
```

profile of v0, /device:TPU:1, one launch (start us, length us, event | category | flops | bytes accessed | tf_op | source)
XLA Modules:
  0.0 117.6 jit_solution(14409229149390299726)
XLA Ops:
  0.6 0.0 copy-start.4
  0.6 0.9 multiply_bitcast_fusion
  1.5 0.0 copy-start.3
  1.5 0.0 copy-start.2
  1.6 0.0 copy-start.1
  1.6 0.0 copy-start
  1.6 0.1 pad_maximum_fusion.2
  1.7 0.0 copy-start.5
  1.7 0.0 copy-done.4
  1.8 0.6 copy-done.3
  2.4 0.0 copy-done.2
  2.4 0.1 copy-done.1
  2.5 0.1 copy-done
  2.6 0.0 copy-done.5
  2.6 110.9 %shard_map.118 = (f32[8,16,192]{2,1,0:T(8,128)S(1)}, f32[8,16,192]{2,1,0:T(8,128)S(1)}, f32[4,8,16,16]{3,2,1,0:T(8,128)S(1)}, f32[4,8,16,16]{3,2,1,0:T(8,128)S(1)}, f32[32,8,128]{2,1,0:T(8,128)S(1)}) custom-call(bf16[8,16,192]{2,1,0:T(8,128)(2,1)S(1)} %copy-done.2, bf16[8,16,192]{2,1,0:T(8,128)(2,1)S(1)} %copy-done.3, bf16[8,16,192]{2,1,0:T(8,128)(2,1)S(1)} %copy-done.4, ...), custom_call_target="tpu_custom_call" | custom-call | tf_op jit(solution)/shard_map/pallas_call | solution.py:492
  113.5 0.6 pad_maximum_fusion.3
  114.1 0.1 reshape_squeeze.3
  114.2 0.6 pad_maximum_fusion.1
  114.9 0.7 copy.34
  115.5 0.7 copy.35
  116.2 0.7 copy.36
  116.9 0.7 copy.37
  (11 shorter events, 0.1 us)
Async XLA Ops:
  0.6 1.1 copy-start.4
  1.5 0.8 copy-start.3
  1.5 0.9 copy-start.2
  1.6 0.9 copy-start.1
  1.6 1.0 copy-start
  1.7 0.9 copy-start.5
where the time goes:
time: 118 us
  Pallas kernels  111 us (94%)
  local copies, waits for them, and re-layouts  3.72 us (3%)
  other arithmetic  2.21 us (2%)
    pallas_call x1, Pallas kernels, on_device(): pl.pallas_call(body, out_shape=[jax.ShapeDtypeStruct((8, 16, 192), F32),...  111 us
    unnamed x16, local copies, waits for them, and re-layouts  3.55 us

commit v1 on v0

v1 whole, which is shorter than its diff:
```python
import functools
import math

import jax
import jax.numpy as jnp
from jax import lax
from jax.experimental import pallas as pl
from jax.experimental.pallas import tpu as pltpu
from jax.sharding import PartitionSpec as P

F32 = jnp.float32
T = 16
PAIRS = 8
LOG2E = 1.4426950408889634
LN2 = 0.6931471805599453
COLS = 32
ROWS = 8


def low_half():
    return lax.broadcasted_iota(jnp.int32, (8, 128), 1) < 64


def fold(q, low):
    return jnp.where(low, q[0], q[1]) + q[2], jnp.where(low, q[1], q[0])


def tri(f, *groups):
    return [f(*parts) for parts in zip(*groups)]


def add(a, b):
    return a + b


def mul(a, b):
    return a * b


def body(x_ref, s_ref, g_ref, w_ref, r_ref, rt_ref, sk_ref,
         gi_ref, gs_ref, gc_ref, fin_ref,
         flat, zmsg, rowtile, dat_r, dat_z, decays, ssend, srecv, csend, crecv, bsend, brecv,
         zrecv, ztile, keep, acc_r, acc_z, zbuf, pick, place, spread_r, spread_z, shift, nat,
         zout, zback, asend, arecv, zsum, send_sem, recv_sem):
    col = lax.axis_index("cols")
    row = lax.axis_index("rows")
    low = low_half()

    barrier = pltpu.get_barrier_semaphore()

    def greet_cols(i, _):
        pl.semaphore_signal(barrier, inc=1, device_id={"cols": lax.rem(col + i, COLS)},
                            device_id_type=pl.DeviceIdType.MESH)
        return 0

    def greet_rows(i, _):
        pl.semaphore_signal(barrier, inc=1, device_id={"rows": lax.rem(row + i, ROWS)},
                            device_id_type=pl.DeviceIdType.MESH)
        return 0

    lax.fori_loop(1, COLS, greet_cols, 0)
    lax.fori_loop(1, ROWS, greet_rows, 0)

    def remote(src, dst, n, **to):
        return pltpu.make_async_remote_copy(
            src_ref=src, dst_ref=dst, send_sem=send_sem.at[n], recv_sem=recv_sem.at[n],
            device_id=to, device_id_type=pl.DeviceIdType.MESH)

    def taken(ref, sem, n):
        pltpu.make_async_copy(ref, ref, sem.at[n]).wait()

    for r in range(8):
        sv = s_ref[r].astype(F32)
        gv = g_ref[r].astype(F32)
        pv = sv * x_ref[r].astype(F32)
        at = pl.ds(r * 16, 16)
        flat[0, at, :] = sv[:, :128]
        flat[1, at, :] = pv[:, :128]
        flat[2, at, :] = gv[:, :128]
        flat[3, at, :] = jnp.concatenate([sv[:, 128:], pv[:, 128:]], axis=1)
        flat[4, at, :] = jnp.concatenate(
            [gv[:, 128:]] + [ref[k, r].astype(F32) for ref in (w_ref, r_ref) for k in (2, 3)], axis=1)
        flat[5, at, :] = jnp.concatenate(
            [gv[:, 128:]] + [ref[k, r].astype(F32) for ref in (w_ref, r_ref) for k in (0, 1)], axis=1)

    for t in range(T):
        at = pl.ds(t, 8, stride=16)
        for q in range(5):
            zmsg[q, t] = flat[q, at, :]
        rowtile[t] = flat[5, at, :]

    def unpack(dat, t, tiles):
        s_lo, p_lo, g_lo, sp, gc = tiles
        spr = pltpu.roll(sp, 64, 1)
        dat[0, t] = s_lo
        dat[1, t] = jnp.where(low, sp, spr)
        dat[2, t] = p_lo
        dat[3, t] = jnp.where(low, spr, sp)
        dat[4, t] = g_lo
        dat[5, t] = jnp.where(low, gc, pltpu.roll(gc, 64, 1))

    def step_sums(dat):
        lo, hi = dat[0, 0], dat[1, 0]
        for t in range(1, T):
            lo, hi = lo + dat[0, t], hi + dat[1, t]
        return lo, hi

    for t in range(T):
        unpack(dat_r, t, (zmsg[0, t], zmsg[1, t], zmsg[2, t], zmsg[3, t], rowtile[t]))
    ssum = step_sums(dat_r)
    ssend[0] = ssum[0]
    ssend[1] = ssum[1]
    srecv[col] = ssend[...]

    pick_j = lax.broadcasted_iota(jnp.int32, (128, 128), 0)
    pick_up = pick_j - jnp.where(lax.broadcasted_iota(jnp.int32, (128, 128), 1) < 64, 0, 8)

    def fill_pick(p, _):
        for which in range(4):
            base = 64 + 16 * which
            for i, (source, start) in enumerate(((pick_j, base), (pick_j, base + 8), (pick_up, base))):
                pick[p, :, pl.ds((which * 3 + i) * 128, 128)] = jnp.where(
                    source == start + p, 1.0, 0.0).astype(jnp.bfloat16)
        return 0

    lax.fori_loop(0, PAIRS, fill_pick, 0)

    pl.semaphore_wait(barrier, COLS - 1 + ROWS - 1)

    def send_z(i, _):
        to = lax.rem(row + i, ROWS)
        for c in range(2):
            remote(zmsg.at[:, 2 * to + c],
                   zrecv.at[:, pl.ds(pl.multiple_of(c * 64 + row * 8, 8), 8), :], 0, rows=to).start()
        return 0

    lax.fori_loop(1, ROWS, send_z, 0)
    for c in range(2):
        for q in range(5):
            zrecv[q, pl.ds(pl.multiple_of(c * 64 + row * 8, 8), 8), :] = zmsg[q, 2 * row + c]

    def send_s(i, _):
        to = lax.rem(col + i, COLS)
        remote(ssend, srecv.at[col], 1, cols=to).start()
        return 0

    lax.fori_loop(1, COLS, send_s, 0)

    def rates(k, p):
        return [jnp.broadcast_to(rt_ref[k, p, pl.ds(i, 1), :], (8, 128)) for i in range(3)]

    def load(dat, q, t):
        lo = dat[2 * q, t]
        return [lo, lo, dat[2 * q + 1, t]]

    W_A, W_D, R_A, R_D = 0, 1, 2, 3
    zero3 = [jnp.zeros((8, 128), F32)] * 3

    def coefs(wide, slot, t, which):
        return [wide[slot, pl.ds(t * 8, 8), pl.ds((which * 3 + i) * 128, 128)] for i in range(3)]

    def held(t, slot):
        return [decays[slot, t, i] for i in range(3)], [decays[slot, t, 3 + i] for i in range(3)]

    def local_pass(p, slot, dslot, ka, kd, dat, wide, tile):
        wide[slot] = jnp.dot(tile[...], pick[p], preferred_element_type=F32)
        ra, rd = rates(ka, p), rates(kd, p)

        def up(t, carry):
            fa, md = carry[:3], carry[3:]
            s = load(dat, 0, t)
            da = tri(lambda a, b: jnp.exp2(a * b), s, ra)
            dd = tri(lambda a, b: jnp.exp2(a * b), s, rd)
            for i in range(3):
                decays[dslot, t, i] = da[i]
                decays[dslot, t, 3 + i] = dd[i]
            drive = tri(mul, load(dat, 1, t), coefs(wide, slot, t, W_A))
            fa = tri(add, tri(mul, da, fa), drive)
            md = tri(mul, dd, tri(add, tri(mul, load(dat, 2, t), coefs(wide, slot, t, R_D)), md))
            return (*fa, *md)

        def down(i, carry):
            t = T - 1 - i
            ma, fd = carry[:3], carry[3:]
            da, dd = held(t, dslot)
            drive = tri(mul, load(dat, 1, t), coefs(wide, slot, t, W_D))
            fd = tri(add, tri(mul, dd, fd), drive)
            ma = tri(mul, da, tri(add, tri(mul, load(dat, 2, t), coefs(wide, slot, t, R_A)), ma))
            return (*ma, *fd)

        a = lax.fori_loop(0, T, up, (*zero3, *zero3), unroll=True)
        b = lax.fori_loop(0, T, down, (*zero3, *zero3), unroll=True)
        return a[:3], b[:3], b[3:], a[3:]

    def final_pass(p, slot, dslot, ka, kd, dat, wide, acc, starts):
        ra, rd = rates(ka, p), rates(kd, p)
        fa0, ma0, fd0, md0 = starts

        def put(q, t, parts):
            zbuf[q, p, 0, t], zbuf[q, p, 1, t] = fold(parts, low)

        def up(t, carry):
            h, m = carry[:3], carry[3:]
            da, dd = held(t, dslot)
            sx, g = load(dat, 1, t), load(dat, 2, t)
            db = tri(mul, da, h)
            h = tri(add, db, tri(mul, sx, coefs(wide, slot, t, W_A)))
            adj = tri(add, tri(mul, g, coefs(wide, slot, t, R_D)), m)
            for i in range(3):
                keep[t, i] = db[i]
                keep[t, 3 + i] = adj[i]
            put(2, t, tri(mul, h, g))
            put(1, t, tri(mul, adj, sx))
            th = tri(mul, adj, coefs(wide, slot, t, W_D))
            keep[t, 6] = th[0] + th[1]
            keep[t, 7] = th[2]
            return (*h, *tri(mul, dd, adj))

        def down(i, carry):
            t = T - 1 - i
            m, h, acc_a, acc_d = carry[:3], carry[3:6], carry[6:9], carry[9:]
            da, dd = held(t, dslot)
            s, sx, g = load(dat, 0, t), load(dat, 1, t), load(dat, 2, t)
            db = tri(mul, dd, h)
            h = tri(add, db, tri(mul, sx, coefs(wide, slot, t, W_D)))
            adj = tri(add, tri(mul, g, coefs(wide, slot, t, R_A)), m)
            put(3, t, tri(mul, h, g))
            put(0, t, tri(mul, adj, sx))
            th = tri(mul, adj, coefs(wide, slot, t, W_A))
            acc[0, t] += keep[t, 6] + (th[0] + th[1])
            acc[1, t] += keep[t, 7] + th[2]
            mem_a = tri(mul, adj, [keep[t, i] for i in range(3)])
            mem_d = tri(mul, [keep[t, 3 + i] for i in range(3)], db)
            mr = tri(add, tri(mul, mem_a, ra), tri(mul, mem_d, rd))
            acc[2, t] += mr[0] + mr[1]
            acc[3, t] += mr[2]
            acc_a = tri(add, acc_a, tri(mul, mem_a, s))
            acc_d = tri(add, acc_d, tri(mul, mem_d, s))
            return (*tri(mul, da, adj), *h, *acc_a, *acc_d)

        lax.fori_loop(0, T, up, (*fa0, *md0), unroll=True)
        out = lax.fori_loop(0, T, down, (*ma0, *fd0, *zero3, *zero3), unroll=True)
        for k, sums in ((ka, out[6:9]), (kd, out[9:])):
            for i in range(3):
                asend[k * PAIRS + p, pl.ds(i, 1), :] = -jnp.sum(sums[i], axis=0, keepdims=True)

    def channel_sums():
        total = None
        for q in range(4):
            whole = jnp.concatenate(
                [zbuf[q, p, j].reshape(128, 128) for p in range(PAIRS) for j in range(2)], axis=1)
            high = whole.astype(jnp.bfloat16)
            rest = (whole - high.astype(F32)).astype(jnp.bfloat16)
            part = jnp.dot(high, place[q], preferred_element_type=F32)
            part = part + jnp.dot(rest, place[q], preferred_element_type=F32)
            total = part if total is None else total + part
        return total.reshape(T, 8, 128)

    def settle(acc, t):
        th, m = acc[1, t], acc[3, t]
        return jnp.where(low, th, m) + pltpu.roll(jnp.where(low, m, th), 64, 1)

    tile_r = rowtile[...].reshape(128, 128).astype(jnp.bfloat16)
    ztile[...] = tile_r

    def row_local(p, _):
        fa, ma, fd, md = local_pass(p, p, p, 0, 1, dat_r, spread_r, ztile)
        for q, parts in enumerate((fa, ma, fd, md)):
            for i in range(3):
                csend[q * PAIRS + p, i] = parts[i]
        return 0

    lax.fori_loop(0, PAIRS, row_local, 0)

    def send_c(i, _):
        to = lax.rem(col + i, COLS)
        remote(csend.at[to], crecv.at[col], 2, cols=to).start()
        return 0

    lax.fori_loop(1, COLS, send_c, 0)
    crecv[col] = csend[col]

    place_k = lax.broadcasted_iota(jnp.int32, (128, 128), 0) // 64 * 8
    place_n = lax.broadcasted_iota(jnp.int32, (128, 128), 1)

    def fill_place(p, _):
        for q in range(4):
            for j, source in enumerate((place_n - place_k, place_n + place_k - 8)):
                place[q, pl.ds(pl.multiple_of(p * 256 + j * 128, 128), 128), :] = jnp.where(
                    source == 16 * q + p, 1.0, 0.0).astype(jnp.bfloat16)
        return 0

    lax.fori_loop(0, PAIRS, fill_place, 0)
    skip = jnp.zeros((1, 192), F32)
    for r in range(8):
        skip = skip + jnp.sum(g_ref[r].astype(F32) * x_ref[r].astype(F32), axis=0, keepdims=True)
    skip_lo = skip[:, :128]
    skip_hi = jnp.concatenate([skip[:, 128:], skip[:, 128:]], axis=1)
    skip_tile = jnp.concatenate([jnp.zeros((3, 128), F32), skip_lo, skip_hi, jnp.zeros((3, 128), F32)], axis=0)

    def put_skip(o, _):
        asend[o] = skip_tile
        return 0

    lax.fori_loop(0, COLS, put_skip, 0)
    acc_r[...] = jnp.zeros_like(acc_r)
    acc_z[...] = jnp.zeros_like(acc_z)
    shift[...] = jnp.zeros_like(shift)

    taken(srecv.at[pl.ds(0, COLS - 1)], recv_sem, 1)
    taken(crecv.at[pl.ds(0, COLS - 1)], recv_sem, 2)
    kind = col // PAIRS
    pair = lax.rem(col, PAIRS)
    falls = jnp.where((kind == 1) | (kind == 2), 1, 0)
    own_rates = rates(kind // 2, pair)

    def chain(i, carry):
        b = i + falls * (COLS - 1 - 2 * i)
        for j in range(3):
            bsend[b, j] = carry[j]
        s_lo, s_hi = srecv[b, 0], srecv[b, 1]
        kept = tri(lambda a, r: jnp.exp2(a * r), [s_lo, s_lo, s_hi], own_rates)
        return tuple(kept[j] * carry[j] + crecv[b, j] for j in range(3))

    lax.fori_loop(0, COLS, chain, tuple(zero3), unroll=True)

    def send_b(i, _):
        to = lax.rem(col + i, COLS)
        remote(bsend.at[to], brecv.at[col], 3, cols=to).start()
        return 0

    lax.fori_loop(1, COLS, send_b, 0)
    brecv[col] = bsend[col]

    taken(zrecv.at[:, pl.ds(0, 112), :], recv_sem, 0)
    for t in range(T):
        at = pl.ds(t, 8, stride=16)
        tiles = [zrecv[q, at, :] for q in range(5)]
        unpack(dat_z, t, tiles)
        rowtile[t] = tiles[4]
    ztile[...] = rowtile[...].reshape(128, 128).astype(jnp.bfloat16)
    chunk = lax.rem(lax.broadcasted_iota(jnp.int32, (8, 128), 0), 4)
    from_chunk = {1: [chunk >= d for d in (1, 2, 3)], -1: [chunk < 4 - d for d in (1, 2, 3)]}

    def shifted(j, d):
        return shift[j, pl.ds(16 - 2 * d, 8, stride=2), :]

    def set_shift(j, value):
        shift[j, pl.ds(16, 8, stride=2), :] = value

    zs = step_sums(dat_z)
    set_shift(12, zs[0])
    set_shift(13, zs[1])
    moved = tuple(shifted(j, d) for d in (1, 2, -1, -2) for j in (12, 13))

    def line_final(p, moved):
        ends = local_pass(p, 0, PAIRS, 2, 3, dat_z, spread_z, ztile)
        for e, parts in enumerate(ends):
            for i in range(3):
                set_shift(e * 3 + i, parts[i])
        starts = []
        for e, (k, sign) in enumerate(((2, 1), (2, -1), (3, -1), (3, 1))):
            rate = rates(k, p)
            at = 0 if sign == 1 else 4
            near, far = (moved[at], moved[at], moved[at + 1]), (moved[at + 2], moved[at + 2], moved[at + 3])
            start = []
            for i in range(3):
                f1, f2, f3 = (jnp.where(from_chunk[sign][d - 1], shifted(e * 3 + i, d * sign), 0.0)
                              for d in (1, 2, 3))
                start.append(f1 + jnp.exp2(near[i] * rate[i]) * (f2 + jnp.exp2(far[i] * rate[i]) * f3))
            starts.append(start)
        final_pass(p, 0, PAIRS, 2, 3, dat_z, spread_z, acc_z, starts)
        return moved

    lax.fori_loop(0, PAIRS, line_final, moved)
    sums = channel_sums()
    for t in range(T):
        at = pl.ds(t, 8, stride=16)
        zout[0, at, :] = acc_z[0, t]
        zout[1, at, :] = acc_z[2, t]
        zout[2, at, :] = settle(acc_z, t)
        zout[3, at, :] = sums[t]

    def send_back(i, _):
        to = lax.rem(row + i, ROWS)
        for c in range(2):
            remote(zout.at[:, pl.ds(pl.multiple_of(c * 64 + to * 8, 8), 8), :],
                   zback.at[:, pl.ds(pl.multiple_of(row * 16 + c * 8, 8), 8), :], 4, rows=to).start()
        return 0

    lax.fori_loop(1, ROWS, send_back, 0)
    for c in range(2):
        zback[:, pl.ds(pl.multiple_of(row * 16 + c * 8, 8), 8), :] = (
            zout[:, pl.ds(pl.multiple_of(c * 64 + row * 8, 8), 8), :])

    taken(brecv.at[pl.ds(0, COLS - 1)], recv_sem, 3)

    def row_final(p, _):
        starts = [[brecv[q * PAIRS + p, i] for i in range(3)] for q in range(4)]
        final_pass(p, p, p, 0, 1, dat_r, spread_r, acc_r, starts)
        return 0

    lax.fori_loop(0, PAIRS, row_final, 0)

    def send_a(i, _):
        to = lax.rem(col + i, COLS)
        remote(asend.at[to], arecv.at[col], 5, cols=to).start()
        return 0

    lax.fori_loop(1, COLS, send_a, 0)
    arecv[col] = asend[col]

    sums = channel_sums()
    for t in range(T):
        at = pl.ds(t, 8, stride=16)
        nat[0, at, :] = acc_r[0, t]
        nat[1, at, :] = acc_r[2, t]
        nat[2, at, :] = settle(acc_r, t)
        nat[3, at, :] = sums[t]

    taken(arecv.at[pl.ds(0, COLS - 1)], recv_sem, 5)
    total = arecv[0]
    for b in range(1, COLS):
        total = total + arecv[b]
    zsum[row] = total

    def send_zsum(i, _):
        to = lax.rem(row + i, ROWS)
        remote(zsum.at[row], zsum.at[row], 6, rows=to).start()
        return 0

    lax.fori_loop(1, ROWS, send_zsum, 0)
    taken(zsum.at[pl.ds(0, ROWS - 1)], recv_sem, 6)
    total = zsum[0]
    for b in range(1, ROWS):
        total = total + zsum[b]
    fin_ref[col] = total

    def send_fin(i, _):
        to = lax.rem(col + i, COLS)
        remote(fin_ref.at[col], fin_ref.at[col], 7, cols=to).start()
        return 0

    lax.fori_loop(1, COLS, send_fin, 0)

    taken(zback.at[:, pl.ds(0, 112), :], recv_sem, 4)
    for r in range(8):
        back = pl.ds(r, 16, stride=8)
        at = pl.ds(r * 16, 16)
        th_lo = nat[0, at, :] + zback[0, back, :]
        m_lo = nat[1, at, :] + zback[1, back, :]
        packed = nat[2, at, :] + zback[2, back, :]
        th_hi = packed[:, :64]
        m_hi = pltpu.roll(packed, 64, 1)[:, :64]
        xv = x_ref[r].astype(F32)
        sv = s_ref[r].astype(F32)
        gv = g_ref[r].astype(F32)
        gi_ref[r, :, :128] = sk_ref[:, :128] * gv[:, :128] + sv[:, :128] * th_lo
        gi_ref[r, :, 128:] = sk_ref[:, 128:] * gv[:, 128:] + sv[:, 128:] * th_hi
        gs_ref[r, :, :128] = th_lo * xv[:, :128] + LN2 * m_lo
        gs_ref[r, :, 128:] = th_hi * xv[:, 128:] + LN2 * m_hi
        gc_ref[r] = nat[3, at, :] + pltpu.roll(zback[3, back, :], 64, 1)

    taken(fin_ref.at[pl.ds(0, COLS - 1)], recv_sem, 7)

    taken(zrecv.at[:, pl.ds(0, 112), :], send_sem, 0)
    taken(srecv.at[pl.ds(0, COLS - 1)], send_sem, 1)
    taken(crecv.at[pl.ds(0, COLS - 1)], send_sem, 2)
    taken(brecv.at[pl.ds(0, COLS - 1)], send_sem, 3)
    taken(zback.at[:, pl.ds(0, 112), :], send_sem, 4)
    taken(arecv.at[pl.ds(0, COLS - 1)], send_sem, 5)
    taken(zsum.at[pl.ds(0, ROWS - 1)], send_sem, 6)
    taken(fin_ref.at[pl.ds(0, COLS - 1)], send_sem, 7)


def on_device(inputs, step_sizes, write_coef, read_coef, rate_table, skip_gain, grad_out):
    by_state = (rate_table * (-LOG2E)).transpose(0, 2, 1)
    lo = by_state[:, :, :128].reshape(4, 2, 8, 128)
    hi = by_state[:, :, 128:].reshape(4, 2, 8, 64)
    table = jnp.stack([lo[:, 0], lo[:, 1], jnp.concatenate([hi[:, 0], hi[:, 1]], axis=-1)], axis=2)
    vm = pl.BlockSpec(memory_space=pltpu.VMEM)
    B16 = jnp.bfloat16
    scratch = [
        pltpu.VMEM(shape, kind[0] if kind else F32)
        for shape, *kind in (
            ((6, 128, 128),),
            ((5, T, 8, 128),),
            ((T, 8, 128),),
            ((6, T, 8, 128),),
            ((6, T, 8, 128),),
            ((PAIRS + 1, T, 6, 8, 128),),
            ((2, 8, 128),),
            ((COLS, 2, 8, 128),),
            ((COLS, 3, 8, 128),),
            ((COLS, 3, 8, 128),),
            ((COLS, 3, 8, 128),),
            ((COLS, 3, 8, 128),),
            ((5, 128, 128),),
            ((128, 128), B16),
            ((T, 8, 8, 128),),
            ((4, T, 8, 128),),
            ((4, T, 8, 128),),
            ((4, PAIRS, 2, T, 8, 128),),
            ((PAIRS, 128, 12 * 128), B16),
            ((4, PAIRS * 256, 128), B16),
            ((PAIRS, 128, 12 * 128),),
            ((1, 128, 12 * 128),),
            ((14, 40, 128),),
            ((4, 128, 128),),
            ((4, 128, 128),),
            ((4, 128, 128),),
            ((COLS, 8, 128),),
            ((COLS, 8, 128),),
            ((ROWS, 8, 128),),
        )
    ]
    scratch += [pltpu.SemaphoreType.DMA((8,)), pltpu.SemaphoreType.DMA((8,))]
    gi, gs, gc, fin = pl.pallas_call(
        body,
        out_shape=[
            jax.ShapeDtypeStruct((8, 16, 192), F32),
            jax.ShapeDtypeStruct((8, 16, 192), F32),
            jax.ShapeDtypeStruct((8, 16, 128), F32),
            jax.ShapeDtypeStruct((COLS, 8, 128), F32),
        ],
        in_specs=[vm] * 7,
        out_specs=[vm] * 4,
        scratch_shapes=scratch,
        compiler_params=pltpu.CompilerParams(
            collective_id=0, has_side_effects=True, vmem_limit_bytes=48 * 1024 * 1024),
    )(inputs, step_sizes, grad_out, write_coef, read_coef, table, skip_gain.reshape(1, 192))
    parts = fin.reshape(4, 8, 8, 128)
    lo = parts[:, :, :2].transpose(0, 3, 2, 1).reshape(4, 128, 16)
    hi = parts[:, :, 2].reshape(4, 8, 2, 64).transpose(0, 3, 2, 1).reshape(4, 64, 16)
    grad_rates = jnp.concatenate([lo, hi], axis=1)
    grad_skip = jnp.concatenate([fin[0, 3], fin[0, 4, :64]])
    kinds = gc.reshape(8, 16, 2, 2, 2, 16).transpose(3, 2, 4, 0, 1, 5).reshape(2, 4, 8, 16, 16)
    return gi, gs, kinds[0], kinds[1], grad_rates, grad_skip


def solution(mesh):
    cells, coefs = P("rows", "cols", None), P(None, "rows", "cols", None)
    return jax.shard_map(
        on_device, mesh=mesh, in_specs=(cells, cells, coefs, coefs, P(), P(), cells),
        out_specs=(cells, cells, coefs, coefs, P(), P()), check_vma=False)
```

time: 118 us -> 55.1 us (0.47)
  Pallas kernels: 111 us -> 47.2 us
    pallas_call x1, Pallas kernels: 111 us -> 47.2 us  [on_device(): pl.pallas_call(body, out_shape=[jax.ShapeDtypeStruct((8, 16, 192), F32),...]
    slice x0 -> x3, local copies, waits for them, and re-layouts: none -> 1.71 us  [on_device(): return (gi, gs, kinds[0], kinds[1], grad_rates, grad_skip)]
    unnamed x16 -> x14, local copies, waits for them, and re-layouts: 3.55 us -> 2.14 us
where the time goes in v1:
time: 55.1 us; the launch traced here: 55 us
  Pallas kernels  47.2 us (86%)
  local copies, waits for them, and re-layouts  4.74 us (9%)
  other arithmetic  2.21 us (4%)
  between operations  0.79 us (1%)
    pallas_call x1, Pallas kernels, on_device(): pl.pallas_call(body, out_shape=[jax.ShapeDtypeStruct((8, 16, 192), F32),...  47.2 us
    unnamed x14, local copies, waits for them, and re-layouts  2.14 us
    slice x3, local copies, waits for them, and re-layouts, on_device(): return (gi, gs, kinds[0], kinds[1], grad_rates, grad_skip)  1.71 us

profile of v1, /device:TPU:1, one launch (start us, length us, event | category | flops | bytes accessed | tf_op | source)
XLA Modules:
  0.0 55.0 jit_solution(344525310636239392)
XLA Ops:
  0.6 0.0 copy-start.4
  0.6 0.9 %multiply_bitcast_fusion = f32[4,16,192]{2,1,0:T(8,128)S(1)} fusion(f32[4,192,16]{1,2,0:T(8,128)} %param.11), kind=kLoop, calls=%fused_computation.2 | loop fusion | flops 12288 | bytes 98304 | tf_op jit(solution)/shard_map/transpose | solution.py:477
  1.5 0.0 copy-start.3
  1.5 0.0 copy-start.2
  1.6 0.0 copy-start.1
  1.6 0.0 copy-start
  1.6 0.1 pad_maximum_fusion.2
  1.7 0.0 copy-start.5
  1.7 0.0 copy-done.4
  1.8 0.6 %copy-done.3 = bf16[8,16,192]{2,1,0:T(8,128)(2,1)S(1)} copy-done((bf16[8,16,192]{2,1,0:T(8,128)(2,1)S(1)}, bf16[8,16,192]{2,1,0:T(8,128)(2,1)}, u32[]{:S(2)}) %copy-start.3) | copy-done | bytes 49176
  2.4 0.0 copy-done.2
  2.4 0.1 copy-done.1
  2.5 0.1 copy-done
  2.6 0.0 copy-done.5
  2.6 47.2 %shard_map.118 = (f32[8,16,192]{2,1,0:T(8,128)S(1)}, f32[8,16,192]{2,1,0:T(8,128)S(1)}, f32[8,16,128]{2,1,0:T(8,128)S(1)}, f32[32,8,128]{2,1,0:T(8,128)S(1)}) custom-call(bf16[8,16,192]{2,1,0:T(8,128)(2,1)S(1)} %copy-done.2, bf16[8,16,192]{2,1,0:T(8,128)(2,1)S(1)} %copy-done.3, bf16[8,16,192]{2,1,0:T(8,128)(2,1)S(1)} %copy-done.4, ...), custom_call_target="tpu_custom_call" | custom-call | tf_op jit(solution)/shard_map/pallas_call | solution.py:518
  49.8 0.6 %pad_maximum_fusion.3 = f32[192]{0:T(256)} fusion(f32[64]{0:T(128)S(1)} %slice_bitcast_fusion.5, f32[128]{0:T(128)S(1)} %slice_bitcast_fusion.6), kind=kLoop, calls=%fused_computation.12 | loop fusion | flops 192 | bytes 1536 | tf_op jit(solution)/shard_map/concatenate | solution.py:536
  50.5 0.1 reshape_squeeze.3
  50.6 0.6 %pad_maximum_fusion.1 = f32[4,192,16]{1,2,0:T(8,128)} fusion(f32[4,64,16]{1,2,0:T(8,128)S(1)} %bitcast.47, f32[4,128,16]{1,2,0:T(8,128)S(1)} %bitcast.46), kind=kLoop, calls=%fused_computation.1 | loop fusion | flops 12288 | bytes 98304 | tf_op jit(solution)/shard_map/concatenate | solution.py:535
  51.2 0.7 %reshape.41 = f32[8,16,2,2,2,16]{5,4,3,2,1,0:T(2,128)S(1)} reshape(f32[8,16,128]{2,1,0:T(8,128)S(1)} %get-tuple-element.12) | data formatting | bytes 131072 | tf_op jit(solution)/shard_map/reshape | solution.py:537
  51.9 0.3 fusion
  52.2 0.7 %copy.23 = f32[1,2,2,8,16,16]{5,4,3,2,1,0:T(8,128)} copy(f32[1,2,2,8,16,16]{5,2,0,1,4,3:T(2,128)S(1)} %get-tuple-element.14) | data formatting | bytes 65536 | tf_op jit(solution)/shard_map/slice | solution.py:538
  52.9 0.7 %copy.22 = f32[1,2,2,8,16,16]{5,4,3,2,1,0:T(8,128)} copy(f32[1,2,2,8,16,16]{5,2,0,1,4,3:T(2,128)S(1)} %get-tuple-element.15) | data formatting | bytes 65536 | tf_op jit(solution)/shard_map/slice | solution.py:538
  53.6 0.7 %copy.36 = f32[8,16,192]{2,1,0:T(8,128)} copy(f32[8,16,192]{2,1,0:T(8,128)S(1)} %get-tuple-element.26) | data formatting | bytes 196608
  54.3 0.7 %copy.37 = f32[8,16,192]{2,1,0:T(8,128)} copy(f32[8,16,192]{2,1,0:T(8,128)S(1)} %get-tuple-element.27) | data formatting | bytes 196608
  (11 shorter events, 0.1 us)
Async XLA Ops:
  0.6 1.1 %copy-start.4 = (bf16[8,16,192]{2,1,0:T(8,128)(2,1)S(1)}, bf16[8,16,192]{2,1,0:T(8,128)(2,1)}, u32[]{:S(2)}) copy-start(bf16[8,16,192]{2,1,0:T(8,128)(2,1)} %g_ref.1) | copy-start | bytes 147460
  1.5 0.8 %copy-start.3 = (bf16[8,16,192]{2,1,0:T(8,128)(2,1)S(1)}, bf16[8,16,192]{2,1,0:T(8,128)(2,1)}, u32[]{:S(2)}) copy-start(bf16[8,16,192]{2,1,0:T(8,128)(2,1)} %s_ref.1) | copy-start | bytes 147460
  1.5 0.9 %copy-start.2 = (bf16[8,16,192]{2,1,0:T(8,128)(2,1)S(1)}, bf16[8,16,192]{2,1,0:T(8,128)(2,1)}, u32[]{:S(2)}) copy-start(bf16[8,16,192]{2,1,0:T(8,128)(2,1)} %x_ref.1) | copy-start | bytes 147460
  1.6 0.9 %copy-start.1 = (bf16[4,8,16,16]{3,2,1,0:T(8,128)(2,1)S(1)}, bf16[4,8,16,16]{3,2,1,0:T(8,128)(2,1)}, u32[]{:S(2)}) copy-start(bf16[4,8,16,16]{3,2,1,0:T(8,128)(2,1)} %r_ref.1) | copy-start | bytes 49156
  1.6 1.0 %copy-start = (bf16[4,8,16,16]{3,2,1,0:T(8,128)(2,1)S(1)}, bf16[4,8,16,16]{3,2,1,0:T(8,128)(2,1)}, u32[]{:S(2)}) copy-start(bf16[4,8,16,16]{3,2,1,0:T(8,128)(2,1)} %w_ref.1) | copy-start | bytes 49156
  1.7 0.9 %copy-start.5 = (f32[192]{0:T(256)S(1)}, f32[192]{0:T(256)}, u32[]{:S(2)}) copy-start(f32[192]{0:T(256)} %param.12) | copy-start | bytes 2308

commit v2 on v1

--- a/solution.py
+++ b/solution.py
@@ -37,11 +37,17 @@
     return a * b
 
 
-def body(x_ref, s_ref, g_ref, w_ref, r_ref, rt_ref, sk_ref,
-         gi_ref, gs_ref, gc_ref, fin_ref,
+def body(x_in, s_in, g_in, w_in, r_in, rate_in, sk_in,
+         gi_out, gs_out, gw_out, gr_out, rate_out, skip_out,
+         gi_ref, gs_ref, gw_ref, gr_ref, rate_sum, skip_sum, fin_ref,
+         x_ref, s_ref, g_ref, w_ref, r_ref, rate_ref, sk_ref, rt_ref,
          flat, zmsg, rowtile, dat_r, dat_z, decays, ssend, srecv, csend, crecv, bsend, brecv,
-         zrecv, ztile, keep, acc_r, acc_z, zbuf, pick, place, spread_r, spread_z, shift, nat,
-         zout, zback, asend, arecv, zsum, send_sem, recv_sem):
+         zrecv, ztile, keep, acc_r, acc_z, zbuf_r, zbuf_z, pick, place, spread_r, spread_z, shift, nat,
+         zout, zback, asend, arecv, zsum, send_sem, recv_sem, in_sem, out_sem):
+    entries = [pltpu.make_async_copy(src, dst, in_sem.at[i]) for i, (src, dst) in enumerate(
+        ((x_in, x_ref), (s_in, s_ref), (g_in, g_ref), (w_in, w_ref), (r_in, r_ref), (rate_in, rate_ref), (sk_in, sk_ref)))]
+    for entry in entries:
+        entry.start()
     col = lax.axis_index("cols")
     row = lax.axis_index("rows")
     low = low_half()
@@ -69,6 +75,8 @@
     def taken(ref, sem, n):
         pltpu.make_async_copy(ref, ref, sem.at[n]).wait()
 
+    for entry in entries:
+        entry.wait()
     for r in range(8):
         sv = s_ref[r].astype(F32)
         gv = g_ref[r].astype(F32)
@@ -79,9 +87,9 @@
         flat[2, at, :] = gv[:, :128]
         flat[3, at, :] = jnp.concatenate([sv[:, 128:], pv[:, 128:]], axis=1)
         flat[4, at, :] = jnp.concatenate(
-            [gv[:, 128:]] + [ref[k, r].astype(F32) for ref in (w_ref, r_ref) for k in (2, 3)], axis=1)
+            [ref[k, r].astype(F32) for ref in (w_ref, r_ref) for k in (2, 3)] + [gv[:, 128:]], axis=1)
         flat[5, at, :] = jnp.concatenate(
-            [gv[:, 128:]] + [ref[k, r].astype(F32) for ref in (w_ref, r_ref) for k in (0, 1)], axis=1)
+            [ref[k, r].astype(F32) for ref in (w_ref, r_ref) for k in (0, 1)] + [gv[:, 128:]], axis=1)
 
     for t in range(T):
         at = pl.ds(t, 8, stride=16)
@@ -97,13 +105,27 @@
         dat[2, t] = p_lo
         dat[3, t] = jnp.where(low, spr, sp)
         dat[4, t] = g_lo
-        dat[5, t] = jnp.where(low, gc, pltpu.roll(gc, 64, 1))
+        dat[5, t] = jnp.where(low, pltpu.roll(gc, 64, 1), gc)
 
     def step_sums(dat):
         lo, hi = dat[0, 0], dat[1, 0]
         for t in range(1, T):
             lo, hi = lo + dat[0, t], hi + dat[1, t]
         return lo, hi
+
+    pl.semaphore_wait(barrier, COLS - 1 + ROWS - 1)
+
+    def send_z(i, _):
+        to = lax.rem(row + i, ROWS)
+        for c in range(2):
+            remote(zmsg.at[:, 2 * to + c],
+                   zrecv.at[:, pl.ds(pl.multiple_of(c * 64 + row * 8, 8), 8), :], 0, rows=to).start()
+        return 0
+
+    lax.fori_loop(1, ROWS, send_z, 0)
+    for c in range(2):
+        for q in range(5):
+            zrecv[q, pl.ds(pl.multiple_of(c * 64 + row * 8, 8), 8), :] = zmsg[q, 2 * row + c]
 
     for t in range(T):
         unpack(dat_r, t, (zmsg[0, t], zmsg[1, t], zmsg[2, t], zmsg[3, t], rowtile[t]))
@@ -112,12 +134,19 @@
     ssend[1] = ssum[1]
     srecv[col] = ssend[...]
 
-    pick_j = lax.broadcasted_iota(jnp.int32, (128, 128), 0)
-    pick_up = pick_j - jnp.where(lax.broadcasted_iota(jnp.int32, (128, 128), 1) < 64, 0, 8)
+    def send_s(i, _):
+        to = lax.rem(col + i, COLS)
+        remote(ssend, srecv.at[col], 1, cols=to).start()
+        return 0
+
+    lax.fori_loop(1, COLS, send_s, 0)
+
+    pick_j = lax.broadcasted_iota(jnp.int32, (64, 128), 0)
+    pick_up = pick_j - jnp.where(lax.broadcasted_iota(jnp.int32, (64, 128), 1) < 64, 0, 8)
 
     def fill_pick(p, _):
         for which in range(4):
-            base = 64 + 16 * which
+            base = 16 * which
             for i, (source, start) in enumerate(((pick_j, base), (pick_j, base + 8), (pick_up, base))):
                 pick[p, :, pl.ds((which * 3 + i) * 128, 128)] = jnp.where(
                     source == start + p, 1.0, 0.0).astype(jnp.bfloat16)
@@ -125,29 +154,14 @@
 
     lax.fori_loop(0, PAIRS, fill_pick, 0)
 
-    pl.semaphore_wait(barrier, COLS - 1 + ROWS - 1)
-
-    def send_z(i, _):
-        to = lax.rem(row + i, ROWS)
-        for c in range(2):
-            remote(zmsg.at[:, 2 * to + c],
-                   zrecv.at[:, pl.ds(pl.multiple_of(c * 64 + row * 8, 8), 8), :], 0, rows=to).start()
-        return 0
-
-    lax.fori_loop(1, ROWS, send_z, 0)
-    for c in range(2):
-        for q in range(5):
-            zrecv[q, pl.ds(pl.multiple_of(c * 64 + row * 8, 8), 8), :] = zmsg[q, 2 * row + c]
-
-    def send_s(i, _):
-        to = lax.rem(col + i, COLS)
-        remote(ssend, srecv.at[col], 1, cols=to).start()
-        return 0
-
-    lax.fori_loop(1, COLS, send_s, 0)
+    for k in range(4):
+        early, late = rate_ref[k, :8] * -LOG2E, rate_ref[k, 8:] * -LOG2E
+        rt_ref[k, 0] = early[:, :128]
+        rt_ref[k, 1] = late[:, :128]
+        rt_ref[k, 2] = jnp.concatenate([early[:, 128:], late[:, 128:]], axis=1)
 
     def rates(k, p):
-        return [jnp.broadcast_to(rt_ref[k, p, pl.ds(i, 1), :], (8, 128)) for i in range(3)]
+        return [jnp.broadcast_to(rt_ref[k, i, pl.ds(p, 1), :], (8, 128)) for i in range(3)]
 
     def load(dat, q, t):
         lo = dat[2 * q, t]
@@ -163,7 +177,7 @@
         return [decays[slot, t, i] for i in range(3)], [decays[slot, t, 3 + i] for i in range(3)]
 
     def local_pass(p, slot, dslot, ka, kd, dat, wide, tile):
-        wide[slot] = jnp.dot(tile[...], pick[p], preferred_element_type=F32)
+        wide[slot] = jnp.dot(tile[:, :64], pick[p], preferred_element_type=F32)
         ra, rd = rates(ka, p), rates(kd, p)
 
         def up(t, carry):
@@ -192,7 +206,7 @@
         b = lax.fori_loop(0, T, down, (*zero3, *zero3), unroll=True)
         return a[:3], b[:3], b[3:], a[3:]
 
-    def final_pass(p, slot, dslot, ka, kd, dat, wide, acc, starts):
+    def final_pass(p, slot, dslot, ka, kd, dat, wide, acc, zbuf, starts):
         ra, rd = rates(ka, p), rates(kd, p)
         fa0, ma0, fd0, md0 = starts
 
@@ -244,7 +258,7 @@
             for i in range(3):
                 asend[k * PAIRS + p, pl.ds(i, 1), :] = -jnp.sum(sums[i], axis=0, keepdims=True)
 
-    def channel_sums():
+    def channel_sums(zbuf):
         total = None
         for q in range(4):
             whole = jnp.concatenate(
@@ -270,7 +284,7 @@
                 csend[q * PAIRS + p, i] = parts[i]
         return 0
 
-    lax.fori_loop(0, PAIRS, row_local, 0)
+    lax.fori_loop(0, PAIRS, row_local, 0, unroll=2)
 
     def send_c(i, _):
         to = lax.rem(col + i, COLS)
@@ -369,11 +383,28 @@
                               for d in (1, 2, 3))
                 start.append(f1 + jnp.exp2(near[i] * rate[i]) * (f2 + jnp.exp2(far[i] * rate[i]) * f3))
             starts.append(start)
-        final_pass(p, 0, PAIRS, 2, 3, dat_z, spread_z, acc_z, starts)
+        final_pass(p, 0, PAIRS, 2, 3, dat_z, spread_z, acc_z, zbuf_z, starts)
         return moved
 
-    lax.fori_loop(0, PAIRS, line_final, moved)
-    sums = channel_sums()
+    lax.fori_loop(0, PAIRS, line_final, moved, unroll=2)
+    taken(brecv.at[pl.ds(0, COLS - 1)], recv_sem, 3)
+
+    def row_final(p, _):
+        starts = [[brecv[q * PAIRS + p, i] for i in range(3)] for q in range(4)]
+        final_pass(p, p, p, 0, 1, dat_r, spread_r, acc_r, zbuf_r, starts)
+        return 0
+
+    lax.fori_loop(0, PAIRS, row_final, 0, unroll=2)
+
+    def send_a(i, _):
+        to = lax.rem(col + i, COLS)
+        remote(asend.at[to], arecv.at[col], 5, cols=to).start()
+        return 0
+
+    lax.fori_loop(1, COLS, send_a, 0)
+    arecv[col] = asend[col]
+
+    sums = channel_sums(zbuf_z)
     for t in range(T):
         at = pl.ds(t, 8, stride=16)
         zout[0, at, :] = acc_z[0, t]
@@ -393,24 +424,20 @@
         zback[:, pl.ds(pl.multiple_of(row * 16 + c * 8, 8), 8), :] = (
             zout[:, pl.ds(pl.multiple_of(c * 64 + row * 8, 8), 8), :])
 
-    taken(brecv.at[pl.ds(0, COLS - 1)], recv_sem, 3)
-
-    def row_final(p, _):
-        starts = [[brecv[q * PAIRS + p, i] for i in range(3)] for q in range(4)]
-        final_pass(p, p, p, 0, 1, dat_r, spread_r, acc_r, starts)
-        return 0
-
-    lax.fori_loop(0, PAIRS, row_final, 0)
-
-    def send_a(i, _):
-        to = lax.rem(col + i, COLS)
-        remote(asend.at[to], arecv.at[col], 5, cols=to).start()
-        return 0
-
-    lax.fori_loop(1, COLS, send_a, 0)
-    arecv[col] = asend[col]
-
-    sums = channel_sums()
+    taken(arecv.at[pl.ds(0, COLS - 1)], recv_sem, 5)
+    total = arecv[0]
+    for b in range(1, COLS):
+        total = total + arecv[b]
+    zsum[row] = total
+
+    def send_zsum(i, _):
+        to = lax.rem(row + i, ROWS)
+        remote(zsum.at[row], zsum.at[row], 6, rows=to).start()
+        return 0
+
+    lax.fori_loop(1, ROWS, send_zsum, 0)
+
+    sums = channel_sums(zbuf_r)
     for t in range(T):
         at = pl.ds(t, 8, stride=16)
         nat[0, at, :] = acc_r[0, t]
@@ -418,18 +445,6 @@
         nat[2, at, :] = settle(acc_r, t)
         nat[3, at, :] = sums[t]
 
-    taken(arecv.at[pl.ds(0, COLS - 1)], recv_sem, 5)
-    total = arecv[0]
-    for b in range(1, COLS):
-        total = total + arecv[b]
-    zsum[row] = total
-
-    def send_zsum(i, _):
-        to = lax.rem(row + i, ROWS)
-        remote(zsum.at[row], zsum.at[row], 6, rows=to).start()
-        return 0
-
-    lax.fori_loop(1, ROWS, send_zsum, 0)
     taken(zsum.at[pl.ds(0, ROWS - 1)], recv_sem, 6)
     total = zsum[0]
     for b in range(1, ROWS):
@@ -459,9 +474,30 @@
         gi_ref[r, :, 128:] = sk_ref[:, 128:] * gv[:, 128:] + sv[:, 128:] * th_hi
         gs_ref[r, :, :128] = th_lo * xv[:, :128] + LN2 * m_lo
         gs_ref[r, :, 128:] = th_hi * xv[:, 128:] + LN2 * m_hi
-        gc_ref[r] = nat[3, at, :] + pltpu.roll(zback[3, back, :], 64, 1)
+        for first, sums in ((0, nat[3, at, :]), (2, zback[3, back, :])):
+            for j in range(2):
+                gw_ref[first + j, r] = sums[:, 16 * j : 16 * j + 16]
+                gr_ref[first + j, r] = sums[:, 32 + 16 * j : 48 + 16 * j]
+
+    leaving = [pltpu.make_async_copy(src, dst, out_sem.at[i]) for i, (src, dst) in enumerate(
+        ((gi_ref, gi_out), (gs_ref, gs_out), (gw_ref, gw_out), (gr_ref, gr_out)))]
+    for copy in leaving:
+        copy.start()
 
     taken(fin_ref.at[pl.ds(0, COLS - 1)], recv_sem, 7)
+    for k in range(4):
+        lo, late, hi = (jnp.concatenate([fin_ref[k * PAIRS + p, pl.ds(i, 1), :] for p in range(PAIRS)], axis=0)
+                        for i in range(3))
+        rate_sum[k, :8, :128] = lo
+        rate_sum[k, 8:, :128] = late
+        rate_sum[k, :8, 128:] = hi[:, :64]
+        rate_sum[k, 8:, 128:] = hi[:, 64:]
+    skip_sum[:, :128] = fin_ref[0, 3:4, :]
+    skip_sum[:, 128:] = fin_ref[0, 4:5, :64]
+    last = [pltpu.make_async_copy(rate_sum, rate_out, out_sem.at[4]),
+            pltpu.make_async_copy(skip_sum, skip_out, out_sem.at[5])]
+    for copy in last:
+        copy.start()
 
     taken(zrecv.at[:, pl.ds(0, 112), :], send_sem, 0)
     taken(srecv.at[pl.ds(0, COLS - 1)], send_sem, 1)
@@ -471,18 +507,43 @@
     taken(arecv.at[pl.ds(0, COLS - 1)], send_sem, 5)
     taken(zsum.at[pl.ds(0, ROWS - 1)], send_sem, 6)
     taken(fin_ref.at[pl.ds(0, COLS - 1)], send_sem, 7)
+    for copy in leaving + last:
+        copy.wait()
+
+
+def leave(*refs):
+    ins, outs, held, sems = refs[:6], refs[6:12], refs[12:18], refs[18]
+    arrive = [pltpu.make_async_copy(ins[i], held[i], sems.at[i]) for i in range(6)]
+    depart = [pltpu.make_async_copy(held[i], outs[i], sems.at[6 + i]) for i in range(6)]
+    for copy in arrive:
+        copy.start()
+    for i in range(6):
+        arrive[i].wait()
+        depart[i].start()
+    for copy in depart:
+        copy.wait()
 
 
 def on_device(inputs, step_sizes, write_coef, read_coef, rate_table, skip_gain, grad_out):
-    by_state = (rate_table * (-LOG2E)).transpose(0, 2, 1)
-    lo = by_state[:, :, :128].reshape(4, 2, 8, 128)
-    hi = by_state[:, :, 128:].reshape(4, 2, 8, 64)
-    table = jnp.stack([lo[:, 0], lo[:, 1], jnp.concatenate([hi[:, 0], hi[:, 1]], axis=-1)], axis=2)
-    vm = pl.BlockSpec(memory_space=pltpu.VMEM)
     B16 = jnp.bfloat16
     scratch = [
         pltpu.VMEM(shape, kind[0] if kind else F32)
         for shape, *kind in (
+            ((8, 16, 192),),
+            ((8, 16, 192),),
+            ((4, 8, 16, 16),),
+            ((4, 8, 16, 16),),
+            ((4, 16, 192),),
+            ((1, 192),),
+            ((COLS, 8, 128),),
+            ((8, 16, 192), B16),
+            ((8, 16, 192), B16),
+            ((8, 16, 192), B16),
+            ((4, 8, 16, 16), B16),
+            ((4, 8, 16, 16), B16),
+            ((4, 16, 192),),
+            ((1, 192),),
+            ((4, 3, PAIRS, 128),),
             ((6, 128, 128),),
             ((5, T, 8, 128),),
             ((T, 8, 128),),
@@ -501,7 +562,8 @@
             ((4, T, 8, 128),),
             ((4, T, 8, 128),),
             ((4, PAIRS, 2, T, 8, 128),),
-            ((PAIRS, 128, 12 * 128), B16),
+            ((4, PAIRS, 2, T, 8, 128),),
+            ((PAIRS, 64, 12 * 128), B16),
             ((4, PAIRS * 256, 128), B16),
             ((PAIRS, 128, 12 * 128),),
             ((1, 128, 12 * 128),),
@@ -514,28 +576,29 @@
             ((ROWS, 8, 128),),
         )
     ]
-    scratch += [pltpu.SemaphoreType.DMA((8,)), pltpu.SemaphoreType.DMA((8,))]
-    gi, gs, gc, fin = pl.pallas_call(
+    scratch += [pltpu.SemaphoreType.DMA((8,)), pltpu.SemaphoreType.DMA((8,)), pltpu.SemaphoreType.DMA((7,)), pltpu.SemaphoreType.DMA((6,))]
+    cells = jax.ShapeDtypeStruct((8, 16, 192), F32)
+    kinds = jax.ShapeDtypeStruct((4, 8, 16, 16), F32)
+    shapes = [cells, cells, kinds, kinds, jax.ShapeDtypeStruct((4, 16, 192), F32), jax.ShapeDtypeStruct((1, 192), F32)]
+    hbm = pl.BlockSpec(memory_space=pltpu.MemorySpace.HBM)
+    made = pl.pallas_call(
         body,
-        out_shape=[
-            jax.ShapeDtypeStruct((8, 16, 192), F32),
-            jax.ShapeDtypeStruct((8, 16, 192), F32),
-            jax.ShapeDtypeStruct((8, 16, 128), F32),
-            jax.ShapeDtypeStruct((COLS, 8, 128), F32),
-        ],
-        in_specs=[vm] * 7,
-        out_specs=[vm] * 4,
+        out_shape=shapes,
+        in_specs=[hbm] * 7,
+        out_specs=[hbm] * 6,
         scratch_shapes=scratch,
         compiler_params=pltpu.CompilerParams(
-            collective_id=0, has_side_effects=True, vmem_limit_bytes=48 * 1024 * 1024),
-    )(inputs, step_sizes, grad_out, write_coef, read_coef, table, skip_gain.reshape(1, 192))
-    parts = fin.reshape(4, 8, 8, 128)
-    lo = parts[:, :, :2].transpose(0, 3, 2, 1).reshape(4, 128, 16)
-    hi = parts[:, :, 2].reshape(4, 8, 2, 64).transpose(0, 3, 2, 1).reshape(4, 64, 16)
-    grad_rates = jnp.concatenate([lo, hi], axis=1)
-    grad_skip = jnp.concatenate([fin[0, 3], fin[0, 4, :64]])
-    kinds = gc.reshape(8, 16, 2, 2, 2, 16).transpose(3, 2, 4, 0, 1, 5).reshape(2, 4, 8, 16, 16)
-    return gi, gs, kinds[0], kinds[1], grad_rates, grad_skip
+            collective_id=0, has_side_effects=True, vmem_limit_bytes=60 * 1024 * 1024),
+    )(inputs, step_sizes, grad_out, write_coef, read_coef, rate_table.transpose(0, 2, 1), skip_gain.reshape(1, 192))
+    gi, gs, gw, gr, rate, skip = pl.pallas_call(
+        leave,
+        out_shape=shapes,
+        in_specs=[hbm] * 6,
+        out_specs=[hbm] * 6,
+        scratch_shapes=[pltpu.VMEM(a.shape, F32) for a in shapes] + [pltpu.SemaphoreType.DMA((12,))],
+        compiler_params=pltpu.CompilerParams(vmem_limit_bytes=60 * 1024 * 1024),
+    )(*made)
+    return gi, gs, gw, gr, rate.transpose(0, 2, 1), skip.reshape(192)
 
 
 def solution(mesh):

time: 55.1 us -> 51.9 us (0.942)
  local copies, waits for them, and re-layouts: 4.74 us -> 0 us
  Pallas kernels: 47.2 us -> 51.1 us
  other arithmetic: 2.21 us -> 0 us
    pallas_call x1 -> x2, Pallas kernels: 47.2 us -> 51.1 us  [the longest x1 49.1 us: on_device(): pl.pallas_call(body, out_shape=shapes, in_specs=[hbm] * 7, out_specs=[hbm...]
    unnamed x14 -> x0, local copies, waits for them, and re-layouts: 2.14 us -> none
    slice x5 -> x0, local copies, waits for them, and re-layouts: 1.76 us -> none  [the longest x3 1.71 us: on_device(): return (gi, gs, kinds[0], kinds[1], grad_rates, grad_skip)]
    concatenate x3 -> x0, other arithmetic: 1.28 us -> none  [the longest x1 0.64 us: on_device(): grad_rates = jnp.concatenate([lo, hi], axis=1)]
    transpose x1 -> x0, other arithmetic: 0.88 us -> none  [on_device(): by_state = (rate_table * -LOG2E).transpose(0, 2, 1)]
    reshape x3 -> x0, local copies, waits for them, and re-layouts: 0.71 us -> none  [the longest x1 0.7 us: on_device(): gc.reshape(8, 16, 2, 2, 2, 16).transpose(3, 2, 4, 0, 1, 5)]
where the time goes in v2:
time: 51.9 us; the launch traced here: 51.8 us
  Pallas kernels  51.1 us (98%)
  between operations  0.64 us (1%)
    pallas_call x1, Pallas kernels, on_device(): pl.pallas_call(body, out_shape=shapes, in_specs=[hbm] * 7, out_specs=[hbm...  49.1 us
    pallas_call x1, Pallas kernels, on_device(): pl.pallas_call(leave, out_shape=shapes, in_specs=[hbm] * 6, out_specs=[hb...  1.99 us

profile of v2, /device:TPU:1, one launch (start us, length us, event | category | flops | bytes accessed | tf_op | source)
XLA Modules:
  0.0 51.8 jit_solution(14726280912305355654)
XLA Ops:
  0.6 49.1 %shard_map.118 = (f32[8,16,192]{2,1,0:T(8,128)}, f32[8,16,192]{2,1,0:T(8,128)}, f32[4,8,16,16]{3,2,1,0:T(8,128)}, f32[4,8,16,16]{3,2,1,0:T(8,128)}, f32[4,16,192]{2,1,0:T(8,128)}, /*index=5*/f32[1,192]{1,0:T(1,128)}) custom-call(bf16[8,16,192]{2,1,0:T(8,128)(2,1)} %x_in.1, bf16[8,16,192]{2,1,0:T(8,128)(2,1)} %s_in.1, bf16[8,16,192]{2,1,0:T(8,128)(2,1)} %g_in.1, ...), custom_call_target="tpu_custom_call" | custom-call | tf_op jit(solution)/shard_map/pallas_call | solution.py:584
  49.8 2.0 %shard_map.119 = (f32[8,16,192]{2,1,0:T(8,128)}, f32[8,16,192]{2,1,0:T(8,128)}, f32[4,8,16,16]{3,2,1,0:T(8,128)}, f32[4,8,16,16]{3,2,1,0:T(8,128)}, f32[4,16,192]{2,1,0:T(8,128)}, /*index=5*/f32[1,192]{1,0:T(1,128)}) custom-call(f32[8,16,192]{2,1,0:T(8,128)} %get-tuple-element.18.refs_0_, f32[8,16,192]{2,1,0:T(8,128)} %get-tuple-element.19.refs_1_, ...), custom_call_target="tpu_custom_call" | custom-call | tf_op jit(solution)/shard_map/pallas_call | solution.py:593

commit v3 on v2

--- a/solution.py
+++ b/solution.py
@@ -27,6 +27,12 @@
 
 def tri(f, *groups):
     return [f(*parts) for parts in zip(*groups)]
+
+
+def tree(parts):
+    while len(parts) > 1:
+        parts = [a + b for a, b in zip(parts[::2], parts[1::2])]
+    return parts[0]
 
 
 def add(a, b):
@@ -86,10 +92,18 @@
         flat[1, at, :] = pv[:, :128]
         flat[2, at, :] = gv[:, :128]
         flat[3, at, :] = jnp.concatenate([sv[:, 128:], pv[:, 128:]], axis=1)
-        flat[4, at, :] = jnp.concatenate(
-            [ref[k, r].astype(F32) for ref in (w_ref, r_ref) for k in (2, 3)] + [gv[:, 128:]], axis=1)
-        flat[5, at, :] = jnp.concatenate(
-            [ref[k, r].astype(F32) for ref in (w_ref, r_ref) for k in (0, 1)] + [gv[:, 128:]], axis=1)
+
+    def to_lanes(width, start):
+        r = lax.broadcasted_iota(jnp.int32, (width, 128), 0)
+        c = lax.broadcasted_iota(jnp.int32, (width, 128), 1)
+        return jnp.where(c == r + start, 1.0, 0.0).astype(jnp.bfloat16)
+
+    upper = jnp.dot(g_ref[:, :, 128:].reshape(128, 64), to_lanes(64, 64), preferred_element_type=F32)
+    for q, first in ((4, 2), (5, 0)):
+        tile = upper
+        for which, (ref, k) in enumerate((ref, first + j) for ref in (w_ref, r_ref) for j in range(2)):
+            tile = tile + jnp.dot(ref[k].reshape(128, 16), to_lanes(16, 16 * which), preferred_element_type=F32)
+        flat[q] = tile
 
     for t in range(T):
         at = pl.ds(t, 8, stride=16)
@@ -127,11 +141,11 @@
         for q in range(5):
             zrecv[q, pl.ds(pl.multiple_of(c * 64 + row * 8, 8), 8), :] = zmsg[q, 2 * row + c]
 
-    for t in range(T):
-        unpack(dat_r, t, (zmsg[0, t], zmsg[1, t], zmsg[2, t], zmsg[3, t], rowtile[t]))
-    ssum = step_sums(dat_r)
-    ssend[0] = ssum[0]
-    ssend[1] = ssum[1]
+    s_lo, sp = zmsg[0, 0], zmsg[3, 0]
+    for t in range(1, T):
+        s_lo, sp = s_lo + zmsg[0, t], sp + zmsg[3, t]
+    ssend[0] = s_lo
+    ssend[1] = jnp.where(low, sp, pltpu.roll(sp, 64, 1))
     srecv[col] = ssend[...]
 
     def send_s(i, _):
@@ -140,6 +154,8 @@
         return 0
 
     lax.fori_loop(1, COLS, send_s, 0)
+    for t in range(T):
+        unpack(dat_r, t, (zmsg[0, t], zmsg[1, t], zmsg[2, t], zmsg[3, t], rowtile[t]))
 
     pick_j = lax.broadcasted_iota(jnp.int32, (64, 128), 0)
     pick_up = pick_j - jnp.where(lax.broadcasted_iota(jnp.int32, (64, 128), 1) < 64, 0, 8)
@@ -310,13 +326,9 @@
         skip = skip + jnp.sum(g_ref[r].astype(F32) * x_ref[r].astype(F32), axis=0, keepdims=True)
     skip_lo = skip[:, :128]
     skip_hi = jnp.concatenate([skip[:, 128:], skip[:, 128:]], axis=1)
-    skip_tile = jnp.concatenate([jnp.zeros((3, 128), F32), skip_lo, skip_hi, jnp.zeros((3, 128), F32)], axis=0)
-
-    def put_skip(o, _):
-        asend[o] = skip_tile
-        return 0
-
-    lax.fori_loop(0, COLS, put_skip, 0)
+    asend[...] = jnp.zeros_like(asend)
+    asend[0, 3:4, :] = skip_lo
+    asend[1, 3:4, :] = skip_hi
     acc_r[...] = jnp.zeros_like(acc_r)
     acc_z[...] = jnp.zeros_like(acc_z)
     shift[...] = jnp.zeros_like(shift)
@@ -387,6 +399,19 @@
         return moved
 
     lax.fori_loop(0, PAIRS, line_final, moved, unroll=2)
+    def send_a(first):
+        def one(i, _):
+            to = first + lax.rem(col + i, COLS // 2)
+
+            @pl.when(to != col)
+            def _():
+                remote(asend.at[to], arecv.at[col], 5, cols=to).start()
+            return 0
+
+        lax.fori_loop(0, COLS // 2, one, 0)
+
+    send_a(COLS // 2)
+
     taken(brecv.at[pl.ds(0, COLS - 1)], recv_sem, 3)
 
     def row_final(p, _):
@@ -396,12 +421,7 @@
 
     lax.fori_loop(0, PAIRS, row_final, 0, unroll=2)
 
-    def send_a(i, _):
-        to = lax.rem(col + i, COLS)
-        remote(asend.at[to], arecv.at[col], 5, cols=to).start()
-        return 0
-
-    lax.fori_loop(1, COLS, send_a, 0)
+    send_a(0)
     arecv[col] = asend[col]
 
     sums = channel_sums(zbuf_z)
@@ -425,10 +445,7 @@
             zout[:, pl.ds(pl.multiple_of(c * 64 + row * 8, 8), 8), :])
 
     taken(arecv.at[pl.ds(0, COLS - 1)], recv_sem, 5)
-    total = arecv[0]
-    for b in range(1, COLS):
-        total = total + arecv[b]
-    zsum[row] = total
+    zsum[row] = tree([arecv[b] for b in range(COLS)])
 
     def send_zsum(i, _):
         to = lax.rem(row + i, ROWS)
@@ -446,10 +463,7 @@
         nat[3, at, :] = sums[t]
 
     taken(zsum.at[pl.ds(0, ROWS - 1)], recv_sem, 6)
-    total = zsum[0]
-    for b in range(1, ROWS):
-        total = total + zsum[b]
-    fin_ref[col] = total
+    fin_ref[col] = tree([zsum[b] for b in range(ROWS)])
 
     def send_fin(i, _):
         to = lax.rem(col + i, COLS)
@@ -493,7 +507,7 @@
         rate_sum[k, :8, 128:] = hi[:, :64]
         rate_sum[k, 8:, 128:] = hi[:, 64:]
     skip_sum[:, :128] = fin_ref[0, 3:4, :]
-    skip_sum[:, 128:] = fin_ref[0, 4:5, :64]
+    skip_sum[:, 128:] = fin_ref[1, 3:4, :64]
     last = [pltpu.make_async_copy(rate_sum, rate_out, out_sem.at[4]),
             pltpu.make_async_copy(skip_sum, skip_out, out_sem.at[5])]
     for copy in last:
@@ -535,7 +549,7 @@
             ((4, 8, 16, 16),),
             ((4, 16, 192),),
             ((1, 192),),
-            ((COLS, 8, 128),),
+            ((COLS, 4, 128),),
             ((8, 16, 192), B16),
             ((8, 16, 192), B16),
             ((8, 16, 192), B16),
@@ -571,9 +585,9 @@
             ((4, 128, 128),),
             ((4, 128, 128),),
             ((4, 128, 128),),
-            ((COLS, 8, 128),),
-            ((COLS, 8, 128),),
-            ((ROWS, 8, 128),),
+            ((COLS, 4, 128),),
+            ((COLS, 4, 128),),
+            ((ROWS, 4, 128),),
         )
     ]
     scratch += [pltpu.SemaphoreType.DMA((8,)), pltpu.SemaphoreType.DMA((8,)), pltpu.SemaphoreType.DMA((7,)), pltpu.SemaphoreType.DMA((6,))]

time: 51.9 us -> 51.1 us (0.985)
  Pallas kernels: 51.1 us -> 50.4 us
    pallas_call x1, Pallas kernels: 49.1 us -> 48.4 us  [on_device(): pl.pallas_call(body, out_shape=shapes, in_specs=[hbm] * 7, out_specs=[hbm...]
where the time goes in v3:
time: 51.1 us; the launch traced here: 51 us
  Pallas kernels  50.4 us (99%)
  between operations  0.64 us (1%)
    pallas_call x1, Pallas kernels, on_device(): pl.pallas_call(body, out_shape=shapes, in_specs=[hbm] * 7, out_specs=[hbm...  48.4 us
    pallas_call x1, Pallas kernels, on_device(): pl.pallas_call(leave, out_shape=shapes, in_specs=[hbm] * 6, out_specs=[hb...  1.99 us

profile of v3, /device:TPU:1, one launch (start us, length us, event | category | flops | bytes accessed | tf_op | source)
XLA Modules:
  0.0 51.0 jit_solution(7293567222961371361)
XLA Ops:
  0.6 48.4 %shard_map.118 = (f32[8,16,192]{2,1,0:T(8,128)}, f32[8,16,192]{2,1,0:T(8,128)}, f32[4,8,16,16]{3,2,1,0:T(8,128)}, f32[4,8,16,16]{3,2,1,0:T(8,128)}, f32[4,16,192]{2,1,0:T(8,128)}, /*index=5*/f32[1,192]{1,0:T(1,128)}) custom-call(bf16[8,16,192]{2,1,0:T(8,128)(2,1)} %x_in.1, bf16[8,16,192]{2,1,0:T(8,128)(2,1)} %s_in.1, bf16[8,16,192]{2,1,0:T(8,128)(2,1)} %g_in.1, ...), custom_call_target="tpu_custom_call" | custom-call | tf_op jit(solution)/shard_map/pallas_call | solution.py:598
  49.0 2.0 %shard_map.119 = (f32[8,16,192]{2,1,0:T(8,128)}, f32[8,16,192]{2,1,0:T(8,128)}, f32[4,8,16,16]{3,2,1,0:T(8,128)}, f32[4,8,16,16]{3,2,1,0:T(8,128)}, f32[4,16,192]{2,1,0:T(8,128)}, /*index=5*/f32[1,192]{1,0:T(1,128)}) custom-call(f32[8,16,192]{2,1,0:T(8,128)} %get-tuple-element.18.refs_0_, f32[8,16,192]{2,1,0:T(8,128)} %get-tuple-element.19.refs_1_, ...), custom_call_target="tpu_custom_call" | custom-call | tf_op jit(solution)/shard_map/pallas_call | solution.py:607

commit v4 on v3

--- a/solution.py
+++ b/solution.py
@@ -27,6 +27,15 @@
 
 def tri(f, *groups):
     return [f(*parts) for parts in zip(*groups)]
+
+
+def ring(d, n):
+    return min(d, n - d)
+
+
+HOPS = sorted(((dx, dy, dc) for dx in range(4) for dy in range(4) for dc in range(2) if dx or dy or dc),
+              key=lambda d: -(ring(d[0], 4) + ring(d[1], 4)))
+ROW_HOPS = sorted(range(1, ROWS), key=lambda d: -ring(d, ROWS))
 
 
 def tree(parts):
@@ -58,6 +67,10 @@
     row = lax.axis_index("rows")
     low = low_half()
 
+    def col_at(d):
+        return (lax.rem(col // 8 + d[0], 4) * 8 + lax.rem(lax.rem(col // 2, 4) + d[1], 4) * 2
+                + lax.rem(lax.rem(col, 2) + d[2], 2))
+
     barrier = pltpu.get_barrier_semaphore()
 
     def greet_cols(i, _):
@@ -129,14 +142,11 @@
 
     pl.semaphore_wait(barrier, COLS - 1 + ROWS - 1)
 
-    def send_z(i, _):
-        to = lax.rem(row + i, ROWS)
+    for d in ROW_HOPS:
+        to = lax.rem(row + d, ROWS)
         for c in range(2):
             remote(zmsg.at[:, 2 * to + c],
                    zrecv.at[:, pl.ds(pl.multiple_of(c * 64 + row * 8, 8), 8), :], 0, rows=to).start()
-        return 0
-
-    lax.fori_loop(1, ROWS, send_z, 0)
     for c in range(2):
         for q in range(5):
             zrecv[q, pl.ds(pl.multiple_of(c * 64 + row * 8, 8), 8), :] = zmsg[q, 2 * row + c]
@@ -148,12 +158,9 @@
     ssend[1] = jnp.where(low, sp, pltpu.roll(sp, 64, 1))
     srecv[col] = ssend[...]
 
-    def send_s(i, _):
-        to = lax.rem(col + i, COLS)
+    for d in HOPS:
+        to = col_at(d)
         remote(ssend, srecv.at[col], 1, cols=to).start()
-        return 0
-
-    lax.fori_loop(1, COLS, send_s, 0)
     for t in range(T):
         unpack(dat_r, t, (zmsg[0, t], zmsg[1, t], zmsg[2, t], zmsg[3, t], rowtile[t]))
 
@@ -302,12 +309,9 @@
 
     lax.fori_loop(0, PAIRS, row_local, 0, unroll=2)
 
-    def send_c(i, _):
-        to = lax.rem(col + i, COLS)
+    for d in HOPS:
+        to = col_at(d)
         remote(csend.at[to], crecv.at[col], 2, cols=to).start()
-        return 0
-
-    lax.fori_loop(1, COLS, send_c, 0)
     crecv[col] = csend[col]
 
     place_k = lax.broadcasted_iota(jnp.int32, (128, 128), 0) // 64 * 8
@@ -350,12 +354,9 @@
 
     lax.fori_loop(0, COLS, chain, tuple(zero3), unroll=True)
 
-    def send_b(i, _):
-        to = lax.rem(col + i, COLS)
+    for d in HOPS:
+        to = col_at(d)
         remote(bsend.at[to], brecv.at[col], 3, cols=to).start()
-        return 0
-
-    lax.fori_loop(1, COLS, send_b, 0)
     brecv[col] = bsend[col]
 
     taken(zrecv.at[:, pl.ds(0, 112), :], recv_sem, 0)
@@ -432,14 +433,11 @@
         zout[2, at, :] = settle(acc_z, t)
         zout[3, at, :] = sums[t]
 
-    def send_back(i, _):
-        to = lax.rem(row + i, ROWS)
+    for d in ROW_HOPS:
+        to = lax.rem(row + d, ROWS)
         for c in range(2):
             remote(zout.at[:, pl.ds(pl.multiple_of(c * 64 + to * 8, 8), 8), :],
                    zback.at[:, pl.ds(pl.multiple_of(row * 16 + c * 8, 8), 8), :], 4, rows=to).start()
-        return 0
-
-    lax.fori_loop(1, ROWS, send_back, 0)
     for c in range(2):
         zback[:, pl.ds(pl.multiple_of(row * 16 + c * 8, 8), 8), :] = (
             zout[:, pl.ds(pl.multiple_of(c * 64 + row * 8, 8), 8), :])

time: 51.1 us -> 50.6 us (level)
  Pallas kernels: 50.4 us -> 49.8 us
    pallas_call x1, Pallas kernels: 48.4 us -> 47.8 us  [on_device(): pl.pallas_call(body, out_shape=shapes, in_specs=[hbm] * 7, out_specs=[hbm...]
where the time goes in v4:
time: 50.6 us; the launch traced here: 50.5 us
  Pallas kernels  49.8 us (98%)
  between operations  0.64 us (1%)
    pallas_call x1, Pallas kernels, on_device(): pl.pallas_call(body, out_shape=shapes, in_specs=[hbm] * 7, out_specs=[hbm...  47.8 us
    pallas_call x1, Pallas kernels, on_device(): pl.pallas_call(leave, out_shape=shapes, in_specs=[hbm] * 6, out_specs=[hb...  1.99 us

profile of v4, /device:TPU:1, one launch (start us, length us, event | category | flops | bytes accessed | tf_op | source)
XLA Modules:
  0.0 50.5 jit_solution(892751249449296987)
XLA Ops:
  0.6 47.8 %shard_map.118 = (f32[8,16,192]{2,1,0:T(8,128)}, f32[8,16,192]{2,1,0:T(8,128)}, f32[4,8,16,16]{3,2,1,0:T(8,128)}, f32[4,8,16,16]{3,2,1,0:T(8,128)}, f32[4,16,192]{2,1,0:T(8,128)}, /*index=5*/f32[1,192]{1,0:T(1,128)}) custom-call(bf16[8,16,192]{2,1,0:T(8,128)(2,1)} %x_in.1, bf16[8,16,192]{2,1,0:T(8,128)(2,1)} %s_in.1, bf16[8,16,192]{2,1,0:T(8,128)(2,1)} %g_in.1, ...), custom_call_target="tpu_custom_call" | custom-call | tf_op jit(solution)/shard_map/pallas_call | solution.py:596
  48.5 2.0 %shard_map.119 = (f32[8,16,192]{2,1,0:T(8,128)}, f32[8,16,192]{2,1,0:T(8,128)}, f32[4,8,16,16]{3,2,1,0:T(8,128)}, f32[4,8,16,16]{3,2,1,0:T(8,128)}, f32[4,16,192]{2,1,0:T(8,128)}, /*index=5*/f32[1,192]{1,0:T(1,128)}) custom-call(f32[8,16,192]{2,1,0:T(8,128)} %get-tuple-element.18.refs_0_, f32[8,16,192]{2,1,0:T(8,128)} %get-tuple-element.19.refs_1_, ...), custom_call_target="tpu_custom_call" | custom-call | tf_op jit(solution)/shard_map/pallas_call | solution.py:605

commit v5 on v4

--- a/solution.py
+++ b/solution.py
@@ -445,12 +445,9 @@
     taken(arecv.at[pl.ds(0, COLS - 1)], recv_sem, 5)
     zsum[row] = tree([arecv[b] for b in range(COLS)])
 
-    def send_zsum(i, _):
-        to = lax.rem(row + i, ROWS)
+    for d in ROW_HOPS:
+        to = lax.rem(row + d, ROWS)
         remote(zsum.at[row], zsum.at[row], 6, rows=to).start()
-        return 0
-
-    lax.fori_loop(1, ROWS, send_zsum, 0)
 
     sums = channel_sums(zbuf_r)
     for t in range(T):
@@ -463,12 +460,9 @@
     taken(zsum.at[pl.ds(0, ROWS - 1)], recv_sem, 6)
     fin_ref[col] = tree([zsum[b] for b in range(ROWS)])
 
-    def send_fin(i, _):
-        to = lax.rem(col + i, COLS)
+    for d in HOPS:
+        to = col_at(d)
         remote(fin_ref.at[col], fin_ref.at[col], 7, cols=to).start()
-        return 0
-
-    lax.fori_loop(1, COLS, send_fin, 0)
 
     taken(zback.at[:, pl.ds(0, 112), :], recv_sem, 4)
     for r in range(8):

time: 50.6 us -> 50.3 us (level)
  no operation moved by 1% of the time
where the time goes in v5:
time: 50.3 us; the launch traced here: 50.2 us
  Pallas kernels  49.5 us (98%)
  between operations  0.64 us (1%)
    pallas_call x1, Pallas kernels, on_device(): pl.pallas_call(body, out_shape=shapes, in_specs=[hbm] * 7, out_specs=[hbm...  47.5 us
    pallas_call x1, Pallas kernels, on_device(): pl.pallas_call(leave, out_shape=shapes, in_specs=[hbm] * 6, out_specs=[hb...  1.99 us

profile of v5, /device:TPU:1, one launch (start us, length us, event | category | flops | bytes accessed | tf_op | source)
XLA Modules:
  0.0 50.2 jit_solution(1728051991146338130)
XLA Ops:
  0.6 47.5 %shard_map.118 = (f32[8,16,192]{2,1,0:T(8,128)}, f32[8,16,192]{2,1,0:T(8,128)}, f32[4,8,16,16]{3,2,1,0:T(8,128)}, f32[4,8,16,16]{3,2,1,0:T(8,128)}, f32[4,16,192]{2,1,0:T(8,128)}, /*index=5*/f32[1,192]{1,0:T(1,128)}) custom-call(bf16[8,16,192]{2,1,0:T(8,128)(2,1)} %x_in.1, bf16[8,16,192]{2,1,0:T(8,128)(2,1)} %s_in.1, bf16[8,16,192]{2,1,0:T(8,128)(2,1)} %g_in.1, ...), custom_call_target="tpu_custom_call" | custom-call | tf_op jit(solution)/shard_map/pallas_call | solution.py:590
  48.2 2.0 %shard_map.119 = (f32[8,16,192]{2,1,0:T(8,128)}, f32[8,16,192]{2,1,0:T(8,128)}, f32[4,8,16,16]{3,2,1,0:T(8,128)}, f32[4,8,16,16]{3,2,1,0:T(8,128)}, f32[4,16,192]{2,1,0:T(8,128)}, /*index=5*/f32[1,192]{1,0:T(1,128)}) custom-call(f32[8,16,192]{2,1,0:T(8,128)} %get-tuple-element.18.refs_0_, f32[8,16,192]{2,1,0:T(8,128)} %get-tuple-element.19.refs_1_, ...), custom_call_target="tpu_custom_call" | custom-call | tf_op jit(solution)/shard_map/pallas_call | solution.py:599
